TPU v7x, 32 devices: a whole 2x2x4 slice. The times are simulated.
32 devices in a mesh: dp: 16 (over z, y, core), seq: 2 (over x).
Axes of the slice: x: 2, y: 2, z: 4, core: 2. Of those that a mesh axis runs over, the one named last changes fastest.
Arguments:
- latents: bfloat16 [16, 1024, 1152], P('dp', 'seq'), may hold values from -6 to 6
- condition: bfloat16 [16, 1152], P('dp'), may hold values from -6 to 6
- cotangent: bfloat16 [16, 1024, 1152], P('dp', 'seq'), may hold values from -6 to 6
- ada_w: bfloat16 [7962624], P(('dp', 'seq')), may hold values from -0.1875 to 0.1875
- qkv_w: bfloat16 [3981312], P(('dp', 'seq')), may hold values from -0.1875 to 0.1875
- proj_w: bfloat16 [1327104], P(('dp', 'seq')), may hold values from -1.5 to 1.5
- fc1_w: bfloat16 [5308416], P(('dp', 'seq')), may hold values from -0.1875 to 0.1875
- fc2_w: bfloat16 [5308416], P(('dp', 'seq')), may hold values from -0.09375 to 0.09375
- biases: bfloat16 [16128], P(('dp', 'seq')), may hold values from -3 to 3
Outputs:
- output: bfloat16 [16, 1024, 1152], P('dp', 'seq')
- grad_latents: float32 [16, 1024, 1152], P('dp', 'seq')
- grad_condition: float32 [16, 1152], P('dp')
- grad_ada: float32 [7962624], P(('dp', 'seq'))
- grad_qkv: float32 [3981312], P(('dp', 'seq'))
- grad_proj: float32 [1327104], P(('dp', 'seq'))
- grad_fc1: float32 [5308416], P(('dp', 'seq'))
- grad_fc2: float32 [5308416], P(('dp', 'seq'))
- grad_biases: float32 [16128], P(('dp', 'seq'))
All inputs are finite; a program needn't handle non-finite values.
Results may differ from a plain program's by a relative error of at most 0.018.
The roundings to bfloat16 on the way count: a program that leaves them out, or rounds other values in their place, can miss the bound.
Values may be sent and summed in bfloat16 or wider, within the bound.
A program may use at most 384 MiB of HBM per device.

v0:
```python
import jax
import jax.numpy as jnp
from jax import lax
from jax.sharding import PartitionSpec as P

D = 1152
HEADS = 16
HD = 72
FF = 4608


def layer_norm(values):
    centred = values - jnp.mean(values, axis=-1, keepdims=True)
    return centred * lax.rsqrt(jnp.mean(centred * centred, axis=-1, keepdims=True) + 1e-06)


def gelu_tanh(values):
    return jax.nn.gelu(values, approximate=True)


def cross(left, right):
    return lax.dot_general(
        left, right, (((0,), (0,)), ((), ())), preferred_element_type=jnp.float32
    )


def against(left, right):
    return lax.dot_general(
        left, right, (((1,), (1,)), ((), ())), preferred_element_type=jnp.float32
    )


def blocked(flat, height, breadth, n_rows, n_cols):
    return (
        flat.reshape(n_rows, n_cols, height // n_rows, breadth // n_cols)
        .transpose(0, 2, 1, 3)
        .reshape(height, breadth)
    )


def unpack(pieces, n_rows, n_cols):
    b_all = pieces[5].astype(jnp.float32)
    return (
        blocked(pieces[0], D, 6 * D, n_rows, n_cols),
        blocked(pieces[1], D, 3 * D, n_rows, n_cols),
        blocked(pieces[2], D, D, n_rows, n_cols),
        blocked(pieces[3], D, FF, n_rows, n_cols),
        blocked(pieces[4], FF, D, n_rows, n_cols),
        (
            b_all[: 6 * D],
            b_all[6 * D : 8 * D],
            b_all[8 * D : 9 * D],
            b_all[9 * D : 9 * D + FF],
            b_all[9 * D + FF :],
        ),
    )


def body(latents, condition, cotangent, ada_w, qkv_w, proj_w, fc1_w, fc2_w, biases):
    lats, rows, width = latents.shape
    count = lats * rows
    scale = HD ** (-0.5)
    n_rows = lax.axis_size("dp")
    n_cols = lax.axis_size("seq")
    pieces = (
        lax.all_gather(ada_w, ("dp", "seq"), axis=0, tiled=True),
        lax.all_gather(qkv_w, ("dp", "seq"), axis=0, tiled=True),
        lax.all_gather(proj_w, ("dp", "seq"), axis=0, tiled=True),
        lax.all_gather(fc1_w, ("dp", "seq"), axis=0, tiled=True),
        lax.all_gather(fc2_w, ("dp", "seq"), axis=0, tiled=True),
        lax.all_gather(biases, ("dp", "seq"), axis=0, tiled=True),
    )
    w_ada, w_qkv, w_proj, w_up, w_down, bias_parts = unpack(pieces, n_rows, n_cols)
    b_ada, b_qv, b_proj, b_up, b_down = bias_parts
    tokens = latents.astype(jnp.float32)
    cond = condition.astype(jnp.float32)
    act = jax.nn.silu(cond).astype(jnp.bfloat16)
    modul = jnp.dot(act, w_ada, preferred_element_type=jnp.float32) + b_ada
    shift1, scale1, gate1, shift2, scale2, gate2 = [
        modul[:, None, j * D : (j + 1) * D] for j in range(6)
    ]
    norm1 = layer_norm(tokens)
    first = (norm1 * (1.0 + scale1) + shift1).astype(jnp.bfloat16).reshape(count, D)
    qkv = jnp.dot(first, w_qkv, preferred_element_type=jnp.float32)
    query = (qkv[:, :D] + b_qv[:D]).astype(jnp.bfloat16).reshape(lats, rows, HEADS, HD)
    keys_own = qkv[:, D : 2 * D].astype(jnp.bfloat16).reshape(lats, rows, D)
    vals_own = (qkv[:, 2 * D :] + b_qv[D:]).astype(jnp.bfloat16).reshape(lats, rows, D)
    keys_all, vals_all = (
        lax.all_gather(keys_own, "seq", axis=1, tiled=True),
        lax.all_gather(vals_own, "seq", axis=1, tiled=True),
    )
    total = keys_all.shape[1]
    keys_h = keys_all.reshape(lats, total, HEADS, HD)
    vals_h = vals_all.reshape(lats, total, HEADS, HD)
    scores = (
        jnp.einsum("bqhd,bkhd->bhqk", query, keys_h, preferred_element_type=jnp.float32) * scale
    )
    peak = jnp.max(scores, axis=-1, keepdims=True)
    expo = jnp.exp(scores - peak)
    summed = jnp.sum(expo, axis=-1, keepdims=True)
    logsum = peak + jnp.log(summed)
    probs = (expo / summed).astype(jnp.bfloat16)
    mixed = jnp.einsum("bhqk,bkhd->bqhd", probs, vals_h, preferred_element_type=jnp.float32)
    mixed = mixed.astype(jnp.bfloat16).reshape(count, D)
    attn = (jnp.dot(mixed, w_proj, preferred_element_type=jnp.float32) + b_proj).reshape(
        lats, rows, D
    )
    middle = tokens + gate1 * attn
    norm2 = layer_norm(middle)
    second = (norm2 * (1.0 + scale2) + shift2).astype(jnp.bfloat16).reshape(count, D)
    upper = jnp.dot(second, w_up, preferred_element_type=jnp.float32) + b_up
    hidden = gelu_tanh(upper).astype(jnp.bfloat16)
    branch = (jnp.dot(hidden, w_down, preferred_element_type=jnp.float32) + b_down).reshape(
        lats, rows, D
    )
    output = (middle + gate2 * branch).astype(jnp.bfloat16)
    back_pieces = (
        lax.all_gather(ada_w, ("dp", "seq"), axis=0, tiled=True),
        lax.all_gather(qkv_w, ("dp", "seq"), axis=0, tiled=True),
        lax.all_gather(proj_w, ("dp", "seq"), axis=0, tiled=True),
        lax.all_gather(fc1_w, ("dp", "seq"), axis=0, tiled=True),
        lax.all_gather(fc2_w, ("dp", "seq"), axis=0, tiled=True),
        lax.all_gather(biases, ("dp", "seq"), axis=0, tiled=True),
    )
    unpacked = unpack(back_pieces, n_rows, n_cols)
    w_ada = unpacked[0]
    w_qkv = unpacked[1]
    w_proj = unpacked[2]
    w_up = unpacked[3]
    w_down = unpacked[4]
    grad_out = cotangent.astype(jnp.float32)
    d_gate2 = jnp.sum(grad_out * branch, axis=1)
    d_branch = (gate2 * grad_out).astype(jnp.bfloat16).reshape(count, D)
    gb_down = jnp.sum(d_branch.astype(jnp.float32), axis=0)
    d_hidden = against(d_branch, w_down)
    gelu_back = jax.vjp(gelu_tanh, upper)[1]
    d_upper = gelu_back(d_hidden)[0].astype(jnp.bfloat16)
    gb_up = jnp.sum(d_upper.astype(jnp.float32), axis=0)
    d_second = against(d_upper, w_up).reshape(lats, rows, D)
    d_shift2 = jnp.sum(d_second, axis=1)
    d_scale2 = jnp.sum(d_second * norm2, axis=1)
    norm_back2 = jax.vjp(layer_norm, middle)[1]
    d_middle = grad_out + norm_back2(d_second * (1.0 + scale2))[0]
    d_gate1 = jnp.sum(d_middle * attn, axis=1)
    d_attn = (gate1 * d_middle).astype(jnp.bfloat16).reshape(count, D)
    gb_proj = jnp.sum(d_attn.astype(jnp.float32), axis=0)
    d_mixed = against(d_attn, w_proj).astype(jnp.bfloat16).reshape(lats, rows, HEADS, HD)
    again = jnp.einsum("bqhd,bkhd->bhqk", query, keys_h, preferred_element_type=jnp.float32) * scale
    probs_full = jnp.exp(again - logsum)
    d_probs = jnp.einsum("bqhd,bkhd->bhqk", d_mixed, vals_h, preferred_element_type=jnp.float32)
    inner = jnp.sum(d_probs * probs_full, axis=-1, keepdims=True)
    d_scores = (probs_full * (d_probs - inner)).astype(jnp.bfloat16)
    d_query = (
        jnp.einsum("bhqk,bkhd->bqhd", d_scores, keys_h, preferred_element_type=jnp.float32) * scale
    )
    d_query = d_query.astype(jnp.bfloat16).reshape(count, D)
    query_all, dmix_all = (
        lax.all_gather(query, "seq", axis=1, tiled=True),
        lax.all_gather(d_mixed, "seq", axis=1, tiled=True),
    )
    lse_all, inner_all = (
        lax.all_gather(logsum[..., 0], "seq", axis=2, tiled=True),
        lax.all_gather(inner[..., 0], "seq", axis=2, tiled=True),
    )
    keys_loc = keys_own.reshape(lats, rows, HEADS, HD)
    vals_loc = vals_own.reshape(lats, rows, HEADS, HD)
    local_scores = (
        jnp.einsum("bqhd,bkhd->bhqk", query_all, keys_loc, preferred_element_type=jnp.float32)
        * scale
    )
    local_probs = jnp.exp(local_scores - lse_all[..., None])
    local_dp = jnp.einsum("bqhd,bkhd->bhqk", dmix_all, vals_loc, preferred_element_type=jnp.float32)
    local_ds = (local_probs * (local_dp - inner_all[..., None])).astype(jnp.bfloat16)
    d_keys = (
        jnp.einsum("bhqk,bqhd->bkhd", local_ds, query_all, preferred_element_type=jnp.float32)
        * scale
    )
    d_keys = d_keys.astype(jnp.bfloat16).reshape(count, D)
    d_vals = jnp.einsum(
        "bhqk,bqhd->bkhd",
        local_probs.astype(jnp.bfloat16),
        dmix_all,
        preferred_element_type=jnp.float32,
    )
    d_vals = d_vals.astype(jnp.bfloat16).reshape(count, D)
    d_qkv = jnp.concatenate([d_query, d_keys, d_vals], axis=1)
    gb_qv = jnp.concatenate(
        [jnp.sum(d_query.astype(jnp.float32), axis=0), jnp.sum(d_vals.astype(jnp.float32), axis=0)]
    )
    d_first = against(d_qkv, w_qkv).reshape(lats, rows, D)
    d_shift1 = jnp.sum(d_first, axis=1)
    d_scale1 = jnp.sum(d_first * norm1, axis=1)
    norm_back1 = jax.vjp(layer_norm, tokens)[1]
    grad_latents = d_middle + norm_back1(d_first * (1.0 + scale1))[0]
    d_modul = jnp.concatenate([d_shift1, d_scale1, d_gate1, d_shift2, d_scale2, d_gate2], axis=1)
    d_modul = lax.psum(d_modul, "seq").astype(jnp.bfloat16)
    d_act = against(d_modul, w_ada)
    silu_back = jax.vjp(jax.nn.silu, cond)[1]
    grad_condition = silu_back(d_act)[0]
    lefts = (
        lax.all_gather(first, "seq", axis=0, tiled=True),
        lax.all_gather(mixed, "seq", axis=0, tiled=True),
        lax.all_gather(second, "seq", axis=0, tiled=True),
        lax.all_gather(hidden, "seq", axis=0, tiled=True),
    )
    rights = (
        lax.all_to_all(d_qkv, "seq", split_axis=1, concat_axis=0, tiled=True),
        lax.all_to_all(d_attn, "seq", split_axis=1, concat_axis=0, tiled=True),
        lax.all_to_all(d_upper, "seq", split_axis=1, concat_axis=0, tiled=True),
        lax.all_to_all(d_branch, "seq", split_axis=1, concat_axis=0, tiled=True),
    )
    block_cols = 6 * D // n_cols
    modul_cols = lax.dynamic_slice_in_dim(
        d_modul, lax.axis_index("seq") * block_cols, block_cols, 1
    )
    partials = (
        cross(act, modul_cols),
        cross(lefts[0], rights[0]),
        cross(lefts[1], rights[1]),
        cross(lefts[2], rights[2]),
        cross(lefts[3], rights[3]),
    )
    grads = (
        lax.psum_scatter(
            partials[0].astype(jnp.bfloat16), "dp", scatter_dimension=0, tiled=True
        ).astype(jnp.float32),
        lax.psum_scatter(
            partials[1].astype(jnp.bfloat16), "dp", scatter_dimension=0, tiled=True
        ).astype(jnp.float32),
        lax.psum_scatter(
            partials[2].astype(jnp.bfloat16), "dp", scatter_dimension=0, tiled=True
        ).astype(jnp.float32),
        lax.psum_scatter(
            partials[3].astype(jnp.bfloat16), "dp", scatter_dimension=0, tiled=True
        ).astype(jnp.float32),
        lax.psum_scatter(
            partials[4].astype(jnp.bfloat16), "dp", scatter_dimension=0, tiled=True
        ).astype(jnp.float32),
    )
    owner = (lax.axis_index("seq") == 0).astype(jnp.float32)
    gb_ada = jnp.sum(d_modul.astype(jnp.float32), axis=0) * owner
    bias_sum = lax.psum_scatter(
        jnp.concatenate([gb_ada, gb_qv, gb_proj, gb_up, gb_down]),
        ("dp", "seq"),
        scatter_dimension=0,
        tiled=True,
    )
    return (
        output,
        grad_latents,
        grad_condition,
        grads[0].reshape(-1),
        grads[1].reshape(-1),
        grads[2].reshape(-1),
        grads[3].reshape(-1),
        grads[4].reshape(-1),
        bias_sum,
    )


def solution(mesh):
    return jax.shard_map(
        body,
        mesh=mesh,
        in_specs=(
            P("dp", "seq", None),
            P("dp", None),
            P("dp", "seq", None),
            P(("dp", "seq")),
            P(("dp", "seq")),
            P(("dp", "seq")),
            P(("dp", "seq")),
            P(("dp", "seq")),
            P(("dp", "seq")),
        ),
        out_specs=(
            P("dp", "seq", None),
            P("dp", "seq", None),
            P("dp", None),
            P(("dp", "seq")),
            P(("dp", "seq")),
            P(("dp", "seq")),
            P(("dp", "seq")),
            P(("dp", "seq")),
            P(("dp", "seq")),
        ),
        check_vma=False,
    )
```

profile of v0, /device:TPU:0, one launch (start us, length us, event | category | flops | bytes accessed | tf_op | source)
XLA Modules:
  0.0 1539.4 jit_solution(1803012659055905432)
XLA Ops:
  13.3 43.6 %all-reduce = bf16[16128]{0:T(1024)(128)(2,1)S(1)} all-reduce(bf16[16128]{0:T(1024)(128)(2,1)S(1)} %dynamic-update-slice), channel_id=1, replica_groups=mesh['dp'=16,'seq'=2] {'dp','seq'}, use_global_device_ids=true, to_apply=%add | all-reduce | flops 16128 | bytes 64512
  57.7 68.5 %all-gather.44.cloned.1.call-done = bf16[32,1,124416]{2,1,0:T(2,128)(2,1)} async-done(((bf16[1,1,124416]{2,1,0:T(2,128)(2,1)}), bf16[32,1,124416]{2,1,0:T(2,128)(2,1)}) %all-gather.44.cloned.1.call-update) | async-done | bytes 7962640 | tf_op jit(solution)/shard_map/all_gather | solution.py:67
  126.2 167.3 %reduce.28 = bf16[32,124416]{1,0:T(8,128)(2,1)} reduce(bf16[32,1,124416]{2,1,0:T(2,128)(2,1)} %all-gather.44.cloned.1.call-done, bf16[]{:T(256)} %constant.72), dimensions={1}, to_apply=%all-gather.6.reduce_sub_computation | reduce | bytes 15925250 | tf_op jit(solution)/shard_map/all_gather | solution.py:67
  293.5 10.6 reshape.456
  304.1 12.9 copy.62
  317.0 18.0 %reshape.457 = bf16[1152,3456]{1,0:T(8,128)(2,1)} reshape(bf16[16,72,2,1728]{3,2,1,0:T(2,128)(2,1)} %copy.62) | data formatting | bytes 15925248 | tf_op jit(solution)/shard_map/reshape | solution.py:37
  335.0 29.2 %reshape.453 = bf16[16,2,72,3456]{3,2,1,0:T(8,128)(2,1)} reshape(bf16[7962624]{0:T(1024)(128)(2,1)} %all-gather.22.cloned.1.call-done) | data formatting | bytes 31850496 | tf_op jit(solution)/shard_map/reshape | solution.py:35
  364.2 57.7 %copy.61 = bf16[16,72,2,3456]{3,2,1,0:T(2,128)(2,1)S(1)} copy(bf16[16,72,2,3456]{3,1,2,0:T(8,128)(2,1)} %bitcast.176) | data formatting | bytes 31850496 | tf_op jit(solution)/shard_map/transpose | solution.py:36
  433.0 7.8 fusion.60
  450.2 59.2 %reduce.29 = bf16[32,41472]{1,0:T(8,128)(2,1)} reduce(bf16[32,1,41472]{2,1,0:T(2,128)(2,1)} %all-gather.46.cloned.1.call-done, bf16[]{:T(256)} %constant.72), dimensions={1}, to_apply=%all-gather.7.reduce_sub_computation | reduce | bytes 5308418 | tf_op jit(solution)/shard_map/all_gather | solution.py:68
  509.4 5.2 reshape.464
  514.6 5.7 copy.66
  520.3 6.8 reshape.465
  527.0 20.0 %reshape.467 = bf16[16,2,72,2304]{3,2,1,0:T(8,128)(2,1)} reshape(bf16[5308416]{0:T(1024)(128)(2,1)} %all-gather.24.cloned.1.call-done) | data formatting | bytes 21233664 | tf_op jit(solution)/shard_map/reshape | solution.py:35
  547.0 15.3 copy.67
  567.1 19.7 %reshape.469 = bf16[16,2,288,576]{3,2,1,0:T(8,128)(2,1)} reshape(bf16[5308416]{0:T(1024)(128)(2,1)} %all-gather.26.cloned.1.call-done) | data formatting | bytes 21233664 | tf_op jit(solution)/shard_map/reshape | solution.py:35
  586.8 44.8 %copy.68 = bf16[16,288,2,576]{3,2,1,0:T(2,128)(2,1)} copy(bf16[16,288,2,576]{3,1,2,0:T(8,128)(2,1)} %bitcast.180) | data formatting | bytes 21233664 | tf_op jit(solution)/shard_map/transpose | solution.py:36
  631.5 23.0 %reshape.470 = bf16[4608,1152]{1,0:T(8,128)(2,1)} reshape(bf16[16,288,2,576]{3,2,1,0:T(2,128)(2,1)} %copy.68) | data formatting | bytes 21233664 | tf_op jit(solution)/shard_map/reshape | solution.py:37
  662.0 15.6 %multiply_reduce_fusion.1 = (f32[16,512]{1,0:T(8,128)S(1)}, f32[16,512,1024]{2,1,0:T(8,128)}) fusion(bf16[512,16,72]{0,2,1:T(8,128)(2,1)} %bitcast.186, bf16[1024,16,72]{0,2,1:T(8,128)(2,1)S(1)} %bitcast.178), kind=kOutput, calls=%fused_computation.9 | convolution fusion | flops 1224728576 | bytes 37126144 | tf_op jit(solution)/shard_map/bqhd,bkhd->bhqk/dot_general | solution.py:96
  678.2 14.9 fusion
  695.9 15.1 fusion.52
  711.1 5.6 fusion.83
  718.9 13.9 multiply_convert_fusion.5
  732.9 17.7 %convert_reduce_fusion = (f32[4608]{0:T(1024)}, bf16[512,4608]{1,0:T(8,128)(2,1)}) fusion(f32[512,4608]{1,0:T(8,128)} %get-tuple-element.41, f32[4608]{0:T(1024)S(1)} %copy-done.54, bf16[4608,1152]{1,0:T(8,128)(2,1)} %reshape.470, bf16[1,512,1152]{2,1,0:T(8,128)(2,1)S(1)} %copy-done.21), kind=kOutput, calls=%fused_computation.25 | convolution fusion | flops 5490077184 | bytes 25989120 | tf_op jit(solution)/shard_map/dot_general | solution.py:28
  750.6 10.0 fusion.33
  780.5 29.4 %all-gather.2 = f32[16,1024]{1,0:T(8,128)} all-gather(f32[16,512]{1,0:T(8,128)S(1)} %log_add_fusion), channel_id=4, replica_groups=mesh['dp'=16,'seq'=2] {'seq'}, dimensions={1}, use_global_device_ids=true | all-gather | bytes 98304 | tf_op jit(solution)/shard_map/all_gather | solution.py:162
  809.9 23.7 %multiply_reduce_fusion = (f32[16,512]{1,0:T(8,128)S(1)}, f32[16,512,1024]{2,1,0:T(8,128)}) fusion(f32[16,512,1024]{2,1,0:T(8,128)} %get-tuple-element.38, f32[16,512]{1,0:T(8,128)S(1)} %log_add_fusion, bf16[512,16,72]{0,2,1:T(8,128)(2,1)S(1)} %bitcast.190, bf16[1024,16,72]{0,2,1:T(8,128)(2,1)S(1)} %bitcast.188), kind=kOutput, calls=%fused_computation.3 | convolution fusion | flops 1241505792 | bytes 70713344 | tf_op jit(solution)/shard_map/bqhd,bkhd->bhqk/dot_general | solution.py:150
  834.2 5.2 all-gather.3
  840.7 15.0 fusion.39
  855.8 24.5 %convert_reduce_fusion.5 = (f32[16,72]{1,0:T(8,128)}, bf16[16,72,512]{2,1,0:T(8,128)(2,1)S(1)}) fusion(bf16[1024,16,72]{0,2,1:T(8,128)(2,1)S(1)} %bitcast.179, f32[16,512,1024]{2,1,0:T(8,128)} %get-tuple-element.44, f32[16,512,1024]{2,1,0:T(8,128)} %get-tuple-element.38, f32[16,512]{1,0:T(8,128)S(1)} %copy-done.31, f32[16,512]{1,0:T(8,128)S(1)} %copy-done.28), kind=kOutput, calls=%fused_computation.80 | convolution fusion | flops 1252260736 | bytes 70717952 | tf_op jit(solution)/shard_map/bhqk,bkhd->bqhd/dot_general | solution.py:154
  880.4 17.2 %multiply_convert_fusion.6 = bf16[16,72,512]{2,1,0:T(8,128)(2,1)S(1)} fusion(f32[16,1024,512]{2,1,0:T(8,128)} %fusion.39, f32[16,1024]{1,0:T(8,128)S(1)} %all-gather.3, f32[16,1024]{1,0:T(8,128)S(1)} %copy-done.33, bf16[512,16,72]{0,2,1:T(8,128)(2,1)} %bitcast.212, bf16[1,1024,16,72]{1,3,2,0:T(8,128)(2,1)} %all-gather.30.cloned.1.call-done, ...), kind=kOutput, calls=%fused_computation.82 | convolution fusion | flops 2459041792 | bytes 40763392 | tf_op jit(solution)/shard_map/bhqk,bqhd->bkhd/dot_general | solution.py:175
  897.6 16.5 %convert_reduce_fusion.4 = (f32[16,72]{1,0:T(8,128)}, bf16[16,72,512]{2,1,0:T(8,128)(2,1)S(1)}) fusion(f32[16,1024,512]{2,1,0:T(8,128)} %fusion.39, f32[16,1024]{1,0:T(8,128)S(1)} %copy-done.33, bf16[1,1024,16,72]{1,3,2,0:T(8,128)(2,1)} %all-gather.30.cloned.1.call-done), kind=kOutput, calls=%fused_computation.79 | convolution fusion | flops 1234893696 | bytes 37163520 | tf_op jit(solution)/shard_map/bhqk,bqhd->bkhd/dot_general | solution.py:179
  929.1 49.4 %all-to-all-done = bf16[512,2,1728]{0,2,1:T(8,128)(2,1)S(1)} async-done(((bf16[512,2,1728]{0,2,1:T(8,128)(2,1)}), bf16[512,2,1728]{0,2,1:T(8,128)(2,1)S(1)}, u32[]{:S(2)}, u32[]{:S(2)}) %all-to-all-start) | async-done | bytes 3538976 | tf_op jit(solution)/shard_map/all_to_all | solution.py:207
  982.3 9.3 convolution_convert_fusion.2
  994.3 107.6 %all_to_all.76 = bf16[512,2,2304]{2,0,1:T(8,128)(2,1)} all-to-all(bf16[512,2,2304]{2,0,1:T(8,128)(2,1)S(1)} %bitcast.184), channel_id=1, replica_groups=mesh['dp'=16,'seq'=2] {'seq'}, dimensions={1} | all-to-all | bytes 9437184 | tf_op jit(solution)/shard_map/all_to_all | solution.py:209
  1101.9 10.5 convolution_convert_fusion
  1116.2 10.7 fusion.26
  1134.7 14.9 fusion.28
  1152.0 10.9 psum.7
  1163.0 5.3 multiply_convert_fusion.4
  1170.2 13.8 all_to_all.77
  1184.2 13.1 convolution_convert_fusion.1
  1198.3 40.9 %all-reduce.3 = f32[16128]{0:T(1024)S(1)} all-reduce(f32[16128]{0:T(1024)S(1)} %constant_dynamic-update-slice_fusion.7), channel_id=13, replica_groups=mesh['dp'=16,'seq'=2] {'dp','seq'}, use_global_device_ids=true, to_apply=%region_28.29.clone | all-reduce | flops 16128 | bytes 129024
  1239.8 10.5 fusion.65
  1252.1 5.2 reduce-scatter.10.cloned.1.call-done
  1259.3 80.6 %reduce-scatter.12.cloned.1.call-done = bf16[72,2304]{1,0:T(8,128)(2,1)} async-done(((bf16[1152,2304]{1,0:T(8,128)(2,1)}), bf16[72,2304]{1,0:T(8,128)(2,1)}) %reduce-scatter.12.cloned.1.call-update) | async-done | bytes 331792 | tf_op jit(solution)/shard_map/reduce_scatter | solution.py:233
  1342.1 101.3 %reduce-scatter.16.cloned.1.call-done = bf16[72,3456]{1,0:T(8,128)(2,1)} async-done(((bf16[1152,3456]{1,0:T(8,128)(2,1)}), bf16[72,3456]{1,0:T(8,128)(2,1)}) %reduce-scatter.16.cloned.1.call-update) | async-done | bytes 497680
  1446.0 84.2 %reduce-scatter.14.cloned.1.call-done = bf16[288,576]{1,0:T(8,128)(2,1)} async-done(((bf16[4608,576]{1,0:T(8,128)(2,1)}), bf16[288,576]{1,0:T(8,128)(2,1)}) %reduce-scatter.14.cloned.1.call-update) | async-done | bytes 331792 | tf_op jit(solution)/shard_map/reduce_scatter | solution.py:236
  (264 shorter events, 116.3 us)
Async XLA Ops:
  7.2 49.8 %copy-start.5 = (bf16[1,512,1152]{2,1,0:T(8,128)(2,1)S(1)}, bf16[1,512,1152]{2,1,0:T(8,128)(2,1)}, u32[]{:S(2)}) copy-start(bf16[1,512,1152]{2,1,0:T(8,128)(2,1)} %param.9) | copy-start | bytes 3538948
  7.2 119.0 %all-gather.44.cloned.1.call-start = ((), (), s32[]{:S(2)}) async-start(), calls=%async_computation.23 | async-start | bytes 16422912 | tf_op jit(solution)/shard_map/all_gather | solution.py:67
  9.3 325.7 %all-gather.22.cloned.1.call-start = ((), (), s32[]{:S(2)}) async-start(), calls=%async_computation.9 | async-start | bytes 16422912 | tf_op jit(solution)/shard_map/all_gather | solution.py:66
  10.1 440.1 %all-gather.46.cloned.1.call-start = ((), (), s32[]{:S(2)}) async-start(), calls=%async_computation.24 | async-start | bytes 5474304 | tf_op jit(solution)/shard_map/all_gather | solution.py:68
  11.8 515.2 %all-gather.24.cloned.1.call-start = ((), (), s32[]{:S(2)}) async-start(), calls=%async_computation.10 | async-start | bytes 10948608 | tf_op jit(solution)/shard_map/all_gather | solution.py:69
  12.4 554.7 %all-gather.26.cloned.1.call-start = ((), (), s32[]{:S(2)}) async-start(), calls=%async_computation.11 | async-start | bytes 10948608 | tf_op jit(solution)/shard_map/all_gather | solution.py:70
  13.0 645.8 %all-gather.38.cloned.1.call-start = ((), (), s32[]{:S(2)}) async-start(), calls=%async_computation.20 | async-start | bytes 3538944 | tf_op jit(solution)/shard_map/all_gather | solution.py:89
  57.2 375.3 %copy-start.39 = (f32[512]{0:T(512)}, f32[512]{0:T(512)S(1)}, u32[]{:S(2)}) copy-start(f32[512]{0:T(512)S(1)} %broadcast_multiply_fusion.1) | copy-start | bytes 6148
  57.6 235.8 %copy-start.57 = (f32[512]{0:T(512)}, f32[512]{0:T(512)S(1)}, u32[]{:S(2)}) copy-start(f32[512]{0:T(512)S(1)} %fusion.25) | copy-start | bytes 6148
  57.7 374.8 %copy-start.41 = (f32[512]{0:T(512)}, f32[512]{0:T(512)S(1)}, u32[]{:S(2)}) copy-start(f32[512]{0:T(512)S(1)} %fusion.72) | copy-start | bytes 6148
  432.5 8.3 copy-start.34
  433.0 7.8 copy-start.23
  444.8 248.3 %all-gather.36.cloned.1.call-start = ((), (), s32[]{:S(2)}) async-start(), calls=%async_computation.19 | async-start | bytes 3538944 | tf_op jit(solution)/shard_map/all_gather | solution.py:90
  449.5 390.0 %all-gather.28.cloned.1.call-start = ((), (), s32[]{:S(2)}) async-start(), calls=%async_computation.12 | async-start | bytes 3538944 | tf_op jit(solution)/shard_map/all_gather | solution.py:158
  658.7 221.7 %all-gather.30.cloned.1.call-start = ((), (), s32[]{:S(2)}) async-start(), calls=%async_computation.13 | async-start | bytes 3538944 | tf_op jit(solution)/shard_map/all_gather | solution.py:159
  662.0 15.6 %copy-start.1 = (bf16[1024,1152]{0,1:T(8,128)(2,1)}, bf16[1024,1152]{0,1:T(8,128)(2,1)S(1)}, u32[]{:S(2)}) copy-start(bf16[1024,1152]{0,1:T(8,128)(2,1)S(1)} %copy.65) | copy-start | bytes 7077892
  695.9 15.1 copy-start.7
  716.6 44.0 %copy-start.3 = (f32[1,512,1152]{2,1,0:T(8,128)}, f32[1,512,1152]{2,1,0:T(8,128)S(1)}, u32[]{:S(2)}) copy-start(f32[1,512,1152]{2,1,0:T(8,128)S(1)} %get-tuple-element.28) | copy-start | bytes 7077892
  718.9 14.0 copy-start.21
  718.9 14.0 copy-start.54
  718.9 31.7 %slice-start = ((s8[10616832]{0:T(1024)(128)(4,1)}), s8[4194304]{0:T(1024)(128)(4,1)S(1)}, s32[]{:S(2)}) async-start(s8[10616832]{0:T(1024)(128)(4,1)} %bitcast.194), calls=%async_computation.27 | async-start | bytes 8388608
  718.9 31.7 %slice-start.1 = ((s8[10616832]{0:T(1024)(128)(4,1)}), s8[4194304]{0:T(1024)(128)(4,1)S(1)}, s32[]{:S(2)}) async-start(s8[10616832]{0:T(1024)(128)(4,1)} %bitcast.194), calls=%async_computation.28 | async-start | bytes 8388608
  732.9 17.7 %slice-start.2 = ((s8[10616832]{0:T(1024)(128)(4,1)}), s8[2228224]{0:T(1024)(128)(4,1)S(1)}, s32[]{:S(2)}) async-start(s8[10616832]{0:T(1024)(128)(4,1)} %bitcast.194), calls=%async_computation.29 | async-start | bytes 4456448
  732.9 17.7 %copy-start.44 = (f32[512]{0:T(512)S(1)}, f32[512]{0:T(512)}, u32[]{:S(2)}) copy-start(f32[512]{0:T(512)} %copy-done.43) | copy-start | bytes 6148
  732.9 17.7 %copy-start.56 = (f32[512]{0:T(512)S(1)}, f32[512]{0:T(512)}, u32[]{:S(2)}) copy-start(f32[512]{0:T(512)} %copy-done.55) | copy-start | bytes 6148
  750.6 10.0 copy-start.59
  769.1 154.8 %all-gather.32.cloned.1.call-start = ((), (), s32[]{:S(2)}) async-start(), calls=%async_computation.15 | async-start | bytes 3538944 | tf_op jit(solution)/shard_map/all_gather | solution.py:202
  769.7 212.6 %all-gather.40.cloned.1.call-start = ((), (), s32[]{:S(2)}) async-start(), calls=%async_computation.21 | async-start | bytes 3538944 | tf_op jit(solution)/shard_map/all_gather | solution.py:201
  770.5 331.5 %all-gather.42.cloned.1.call-start = ((), (), s32[]{:S(2)}) async-start(), calls=%async_computation.22 | async-start | bytes 3538944 | tf_op jit(solution)/shard_map/all_gather | solution.py:203
  774.9 35.1 %copy-start.8 = (bf16[1024,1152]{0,1:T(8,128)(2,1)S(1)}, bf16[1024,1152]{0,1:T(8,128)(2,1)}, u32[]{:S(2)}) copy-start(bf16[1024,1152]{0,1:T(8,128)(2,1)} %copy-done.7) | copy-start | bytes 7077892
  774.9 35.1 %copy-start.9 = (bf16[512,1152]{0,1:T(8,128)(2,1)S(1)}, bf16[512,1152]{0,1:T(8,128)(2,1)}, u32[]{:S(2)}) copy-start(bf16[512,1152]{0,1:T(8,128)(2,1)} %copy.69) | copy-start | bytes 3538948
  774.9 142.1 %all-to-all-start.1 = ((bf16[512,2,576]{0,2,1:T(8,128)(2,1)}), bf16[512,2,576]{0,2,1:T(8,128)(2,1)}, u32[]{:S(2)}, u32[]{:S(2)}) async-start(bf16[512,2,576]{0,2,1:T(8,128)(2,1)} %bitcast.204), calls=%async_computation.2 | async-start | bytes 2359296 | tf_op jit(solution)/shard_map/all_to_all | solution.py:208
  779.7 404.5 %all-gather.34.cloned.1.call-start = ((), (), s32[]{:S(2)}) async-start(), calls=%async_computation.17 | async-start | bytes 14155776 | tf_op jit(solution)/shard_map/all_gather | solution.py:204
  780.5 53.1 %copy-start.27 = (f32[16,512]{1,0:T(8,128)}, f32[16,512]{1,0:T(8,128)S(1)}, u32[]{:S(2)}) copy-start(f32[16,512]{1,0:T(8,128)S(1)} %log_add_fusion) | copy-start | bytes 98308
  840.7 15.0 copy-start.2
  840.7 15.1 copy-start.28
  840.7 15.1 copy-start.31
  855.8 24.6 %copy-start.33 = (f32[16,1024]{1,0:T(8,128)S(1)}, f32[16,1024]{1,0:T(8,128)}, u32[]{:S(2)}) copy-start(f32[16,1024]{1,0:T(8,128)} %all-gather.2) | copy-start | bytes 196612
  880.4 33.7 %copy-start.13 = (bf16[16,72,512]{2,1,0:T(8,128)(2,1)}, bf16[16,72,512]{2,1,0:T(8,128)(2,1)S(1)}, u32[]{:S(2)}) copy-start(bf16[16,72,512]{2,1,0:T(8,128)(2,1)S(1)} %get-tuple-element.48) | copy-start | bytes 3538948
  897.6 16.5 %copy-start.29 = (bf16[16,72,512]{2,1,0:T(8,128)(2,1)}, bf16[16,72,512]{2,1,0:T(8,128)(2,1)S(1)}, u32[]{:S(2)}) copy-start(bf16[16,72,512]{2,1,0:T(8,128)(2,1)S(1)} %multiply_convert_fusion.6) | copy-start | bytes 3538948
  917.0 61.5 %all-to-all-start = ((bf16[512,2,1728]{0,2,1:T(8,128)(2,1)}), bf16[512,2,1728]{0,2,1:T(8,128)(2,1)S(1)}, u32[]{:S(2)}, u32[]{:S(2)}) async-start(bf16[512,2,1728]{0,2,1:T(8,128)(2,1)} %bitcast.42), calls=%async_computation | async-start | bytes 7077888 | tf_op jit(solution)/shard_map/all_to_all | solution.py:207
  921.0 329.4 %reduce-scatter.18.cloned.1.call-start = ((), (), s32[]{:S(2)}) async-start(), calls=%async_computation.26 | async-start | bytes 1566720
  929.1 328.2 %reduce-scatter.10.cloned.1.call-start = ((), (), s32[]{:S(2)}) async-start(), calls=%async_computation.14 | async-start | bytes 4386816 | tf_op jit(solution)/shard_map/reduce_scatter | solution.py:227
  991.6 348.3 %reduce-scatter.12.cloned.1.call-start = ((), (), s32[]{:S(2)}) async-start(), calls=%async_computation.16 | async-start | bytes 5640192 | tf_op jit(solution)/shard_map/reduce_scatter | solution.py:233
  1112.5 330.9 %reduce-scatter.16.cloned.1.call-start = ((), (), s32[]{:S(2)}) async-start(), calls=%async_computation.25 | async-start | bytes 8460288
  1134.7 15.5 %copy-start.51 = (f32[1152]{0:T(1024)S(1)}, f32[1152]{0:T(1024)}, u32[]{:S(2)}) copy-start(f32[1152]{0:T(1024)} %reduce_sum.260) | copy-start | bytes 13828
  1134.7 16.1 %copy-start.62 = (f32[1152]{0:T(1024)S(1)}, f32[1152]{0:T(1024)}, u32[]{:S(2)}) copy-start(f32[1152]{0:T(1024)} %get-tuple-element.9) | copy-start | bytes 13828
  1168.3 361.9 %reduce-scatter.14.cloned.1.call-start = ((), (), s32[]{:S(2)}) async-start(), calls=%async_computation.18 | async-start | bytes 6266880 | tf_op jit(solution)/shard_map/reduce_scatter | solution.py:236
  (40 other events, 112.6 us)
Sparse Core Ops, SparseCore 0:
  11.6 114.5 all-gather.43
  129.1 109.1 all-gather.21
  241.9 63.8 all-gather.45
  308.5 86.2 all-gather.23
  397.6 85.7 all-gather.25
  484.8 34.5 all-gather.37
  521.5 36.0 all-gather.35
  658.8 33.9 all-gather.27
  769.2 47.7 all-gather.29
  818.4 36.7 all-gather.31
  856.8 36.0 all-gather.39
  894.3 43.2 all-gather.41
  939.2 180.7 all-gather.33
  1123.6 58.7 reduce-scatter.17
  1186.1 71.0 reduce-scatter.9
  1261.2 78.7 reduce-scatter.11
  1343.9 99.5 reduce-scatter.15
  1447.7 82.3 reduce-scatter.13
where the time goes:
time: 1550 us; the launch traced here: 1540 us
  waiting for transfers between devices  392 us (25%)
  local copies, waits for them, and re-layouts  336 us (22%)
  other arithmetic  273 us (18%)
  matrix products  261 us (17%)
  blocking collectives  252 us (16%)
    all_gather x1, other arithmetic, body(): lax.all_gather(qkv_w, ('dp', 'seq'), axis=0, tiled=True)  167 us
    transpose x5, local copies, waits for them, and re-layouts, blocked(): return flat.reshape(n_rows, n_cols, height // n_rows, breadth // n_cols)....  136 us
    all_to_all x1, blocking collectives, body(): lax.all_to_all(d_upper, 'seq', split_axis=1, concat_axis=0, tiled=True)  108 us
    unnamed x20, waiting for transfers between devices  104 us
    reshape x5, local copies, waits for them, and re-layouts, blocked(): flat.reshape(n_rows, n_cols, height // n_rows, breadth // n_cols)  84.6 us
    unnamed x2, blocking collectives  84.5 us
    reduce_scatter x1, waiting for transfers between devices, body(): lax.psum_scatter(partials[4].astype(jnp.bfloat16), 'dp', scatter_dimensio...  84.2 us
    reduce_scatter x1, waiting for transfers between devices, body(): lax.psum_scatter(partials[3].astype(jnp.bfloat16), 'dp', scatter_dimensio...  80.6 us
  transfers between devices with their start and end apart: 20, of which 6 were waited for; matrix products, arithmetic and copies ran while one was open for 55% of the time, Pallas kernels for 0%

commit v1 on v0

v1 whole, which is shorter than its diff:
```python
import jax
import jax.numpy as jnp
from jax import lax
from jax.sharding import PartitionSpec as P

D = 1152
HEADS = 16
HD = 72
FF = 4608


def layer_norm(values):
    centred = values - jnp.mean(values, axis=-1, keepdims=True)
    return centred * lax.rsqrt(jnp.mean(centred * centred, axis=-1, keepdims=True) + 1e-06)


def gelu_tanh(values):
    return jax.nn.gelu(values, approximate=True)


def cross(left, right):
    return lax.dot_general(
        left, right, (((0,), (0,)), ((), ())), preferred_element_type=jnp.float32
    )


def against(left, right):
    return lax.dot_general(
        left, right, (((1,), (1,)), ((), ())), preferred_element_type=jnp.float32
    )


def swap(values, axis, stride):
    size = lax.axis_size(axis)
    return lax.ppermute(values, axis, [(d, d ^ stride) for d in range(size)])


def strides_of(size):
    return [1 << b for b in range(size.bit_length() - 1)]


def small_gather(values, axis):
    me = lax.axis_index(axis)
    for stride in strides_of(lax.axis_size(axis)):
        other = swap(values, axis, stride)
        low = (me & stride) == 0
        values = jnp.where(
            low,
            jnp.concatenate([values, other], axis=0),
            jnp.concatenate([other, values], axis=0),
        )
    return values


def halve_rows(values, axis_of, stride, wire):
    bit = (lax.axis_index("dp") // stride) % 2
    axis = axis_of.index(stride)
    send = lax.dynamic_index_in_dim(values, 1 - bit, axis, keepdims=False)
    keep = lax.dynamic_index_in_dim(values, bit, axis, keepdims=False)
    got = swap(send.astype(wire), "dp", stride)
    return (keep.astype(jnp.float32) + got.astype(jnp.float32)).astype(wire)


def reduce_scatter(columns, order, wire):
    n_rows = lax.axis_size("dp")
    axis_of = strides_of(n_rows)[::-1]
    height, width = columns[0].shape
    shape = (2,) * len(axis_of) + (height // n_rows, width)
    state = [c.reshape(shape) for c in columns]
    me_col = lax.axis_index("seq")
    for axis, stride in order:
        if axis == "dp":
            state = [halve_rows(s, axis_of, stride, wire) for s in state]
            axis_of = [s for s in axis_of if s != stride]
        else:
            half = len(state) // 2
            high = ((me_col // half) % 2) == 1
            nxt = []
            for a, b in zip(state[:half], state[half:]):
                send = jnp.where(high, a, b)
                keep = jnp.where(high, b, a)
                got = swap(send.astype(wire), "seq", half)
                nxt.append((keep.astype(jnp.float32) + got.astype(jnp.float32)).astype(wire))
            state = nxt
    return state[0]


def orders():
    rows = [("dp", s) for s in strides_of(lax.axis_size("dp"))]
    cols = [("seq", s) for s in strides_of(lax.axis_size("seq"))[::-1]]
    high = rows[2:][::-1]
    first = rows[:1] + cols + rows[1:2] + high
    second = rows[:1] + rows[1:2] + cols + high
    third = rows[:1] + high + rows[1:2] + cols
    return first, second, third


def shifted(values, shift):
    size = lax.axis_size("seq")
    return lax.ppermute(values, "seq", [(d, (d + shift) % size) for d in range(size)])


def to_heads(values):
    size = lax.axis_size("seq")
    me = lax.axis_index("seq")
    wide = D // size
    parts = values.shape[-1] // D

    def group(g):
        return jnp.concatenate(
            [lax.dynamic_slice_in_dim(values, p * D + g * wide, wide, 2) for p in range(parts)],
            axis=2,
        )

    got = [group(me)]
    for s in range(1, size):
        got.append(shifted(group((me + s) % size), s))
    whole = jnp.concatenate(got, axis=1)
    return [whole[:, :, p * wide : (p + 1) * wide] for p in range(parts)]


def to_tokens(pieces):
    size = lax.axis_size("seq")
    me = lax.axis_index("seq")
    wide = D // size
    parts = len(pieces)
    rows = pieces[0].shape[1] // size
    whole = jnp.concatenate(pieces, axis=2)
    got = [whole[:, :rows]]
    for s in range(1, size):
        got.append(shifted(whole[:, s * rows : (s + 1) * rows], -s))
    out = []
    for p in range(parts):
        mine = [g[:, :, p * wide : (p + 1) * wide] for g in got]
        if size == 2:
            out.append(
                jnp.where(
                    me == 0,
                    jnp.concatenate(mine, axis=2),
                    jnp.concatenate(mine[::-1], axis=2),
                )
            )
        else:
            full = jnp.zeros(whole.shape[:1] + (rows, D), whole.dtype)
            for s in range(size):
                full = lax.dynamic_update_slice_in_dim(
                    full, mine[s], ((me + s) % size) * wide, 2
                )
            out.append(full)
    return jnp.concatenate(out, axis=2)


def attend(query, keys, vals):
    lats, total, wide = query.shape
    heads = wide // HD
    q, k, v = [a.reshape(lats, total, heads, HD) for a in (query, keys, vals)]
    scores = jnp.einsum("bqhd,bkhd->bhqk", q, k, preferred_element_type=jnp.float32) * HD ** (-0.5)
    peak = jnp.max(scores, axis=-1, keepdims=True)
    expo = jnp.exp(scores - peak)
    summed = jnp.sum(expo, axis=-1, keepdims=True)
    logsum = peak + jnp.log(summed)
    probs = (expo / summed).astype(jnp.bfloat16)
    mixed = jnp.einsum("bhqk,bkhd->bqhd", probs, v, preferred_element_type=jnp.float32)
    return mixed.astype(jnp.bfloat16).reshape(lats, total, wide), logsum


def attend_back(query, keys, vals, d_mixed, logsum):
    lats, total, wide = query.shape
    heads = wide // HD
    scale = HD ** (-0.5)
    q, k, v, d = [a.reshape(lats, total, heads, HD) for a in (query, keys, vals, d_mixed)]
    again = jnp.einsum("bqhd,bkhd->bhqk", q, k, preferred_element_type=jnp.float32) * scale
    probs = jnp.exp(again - logsum)
    d_probs = jnp.einsum("bqhd,bkhd->bhqk", d, v, preferred_element_type=jnp.float32)
    inner = jnp.sum(d_probs * probs, axis=-1, keepdims=True)
    d_scores = (probs * (d_probs - inner)).astype(jnp.bfloat16)
    dq = jnp.einsum("bhqk,bkhd->bqhd", d_scores, k, preferred_element_type=jnp.float32) * scale
    dk = jnp.einsum("bhqk,bqhd->bkhd", d_scores, q, preferred_element_type=jnp.float32) * scale
    dv = jnp.einsum(
        "bhqk,bqhd->bkhd", probs.astype(jnp.bfloat16), d, preferred_element_type=jnp.float32
    )
    return [a.astype(jnp.bfloat16).reshape(lats, total, wide) for a in (dq, dk, dv)]


def times(left, columns):
    return jnp.concatenate(
        [jnp.dot(left, c, preferred_element_type=jnp.float32) for c in columns], axis=1
    )


def times_back(left, columns):
    width = columns[0].shape[1]
    return sum(against(left[:, j * width : (j + 1) * width], c) for j, c in enumerate(columns))


def weight_partials(left, right, n_cols):
    width = right.shape[1] // n_cols
    return [
        cross(left, right[:, j * width : (j + 1) * width]).astype(jnp.bfloat16)
        for j in range(n_cols)
    ]


def gathered(flat, height, breadth):
    n_rows, n_cols = lax.axis_size("dp"), lax.axis_size("seq")
    block = flat.reshape(1, height // n_rows, breadth // n_cols)
    whole = lax.all_gather(block, ("dp", "seq"), axis=0, tiled=True)
    whole = whole.reshape(n_rows, n_cols, height // n_rows, breadth // n_cols)
    return [whole[:, j].reshape(height, breadth // n_cols) for j in range(n_cols)]


def body(latents, condition, cotangent, ada_w, qkv_w, proj_w, fc1_w, fc2_w, biases):
    lats, rows, width = latents.shape
    count = lats * rows
    n_rows = lax.axis_size("dp")
    n_cols = lax.axis_size("seq")
    me_row, me_col = lax.axis_index("dp"), lax.axis_index("seq")
    by_x, by_y, by_z = orders()

    share = biases.shape[0]
    payload = jnp.concatenate([biases, condition.reshape(-1)]).reshape(1, -1)
    payload = small_gather(small_gather(payload, "seq"), "dp")
    b_all = payload[:, :share].reshape(-1).astype(jnp.float32)
    conds = payload[:, share:].reshape(n_rows, n_cols, lats, D)[:, 0].reshape(n_rows * lats, D)
    w_qkv = gathered(qkv_w, D, 3 * D)
    w_proj = gathered(proj_w, D, D)
    w_up = gathered(fc1_w, D, FF)
    w_down = gathered(fc2_w, FF, D)
    b_ada = b_all[: 6 * D]
    b_qv = b_all[6 * D : 8 * D]
    b_proj = b_all[8 * D : 9 * D]
    b_up = b_all[9 * D : 9 * D + FF]
    b_down = b_all[9 * D + FF :]

    ada_h, ada_c = D // n_rows, 6 * D // n_cols
    ada_block = ada_w.reshape(ada_h, ada_c)
    acts = jax.nn.silu(conds.astype(jnp.float32)).astype(jnp.bfloat16)
    acts_rows = lax.dynamic_slice_in_dim(acts, me_row * ada_h, ada_h, 1)
    part = jnp.dot(acts_rows, ada_block, preferred_element_type=jnp.float32)
    dp_order = [("dp", s) for s in strides_of(n_rows)[::-1]]
    part = reduce_scatter([part], dp_order, jnp.float32)
    modul = small_gather(part[None], "seq").transpose(1, 0, 2).reshape(lats, 6 * D) + b_ada
    shift1, scale1, gate1, shift2, scale2, gate2 = [
        modul[:, None, j * D : (j + 1) * D] for j in range(6)
    ]

    tokens = latents.astype(jnp.float32)
    norm1 = layer_norm(tokens)
    first = (norm1 * (1.0 + scale1) + shift1).astype(jnp.bfloat16).reshape(count, D)
    b_qkv = jnp.concatenate([b_qv[:D], jnp.zeros((D,), jnp.float32), b_qv[D:]])
    qkv = (times(first, w_qkv) + b_qkv).astype(jnp.bfloat16).reshape(lats, rows, 3 * D)
    query, keys, vals = to_heads(qkv)
    mixed_h, logsum = attend(query, keys, vals)
    mixed = to_tokens([mixed_h]).reshape(count, D)
    attn = (times(mixed, w_proj) + b_proj).reshape(lats, rows, D)
    middle = tokens + gate1 * attn
    norm2 = layer_norm(middle)
    second = (norm2 * (1.0 + scale2) + shift2).astype(jnp.bfloat16).reshape(count, D)
    upper = times(second, w_up) + b_up
    hidden = gelu_tanh(upper).astype(jnp.bfloat16)
    branch = (times(hidden, w_down) + b_down).reshape(lats, rows, D)
    output = (middle + gate2 * branch).astype(jnp.bfloat16)

    grad_out = cotangent.astype(jnp.float32)
    d_gate2 = jnp.sum(grad_out * branch, axis=1)
    d_branch = (gate2 * grad_out).astype(jnp.bfloat16).reshape(count, D)
    gb_down = jnp.sum(d_branch.astype(jnp.float32), axis=0)
    grad_down = reduce_scatter(weight_partials(hidden, d_branch, n_cols), by_x, jnp.bfloat16)
    d_hidden = times_back(d_branch, w_down)
    gelu_back = jax.vjp(gelu_tanh, upper)[1]
    d_upper = gelu_back(d_hidden)[0].astype(jnp.bfloat16)
    gb_up = jnp.sum(d_upper.astype(jnp.float32), axis=0)
    grad_up = reduce_scatter(weight_partials(second, d_upper, n_cols), by_y, jnp.bfloat16)
    d_second = times_back(d_upper, w_up).reshape(lats, rows, D)
    d_shift2 = jnp.sum(d_second, axis=1)
    d_scale2 = jnp.sum(d_second * norm2, axis=1)
    norm_back2 = jax.vjp(layer_norm, middle)[1]
    d_middle = grad_out + norm_back2(d_second * (1.0 + scale2))[0]
    d_gate1 = jnp.sum(d_middle * attn, axis=1)
    d_attn = (gate1 * d_middle).astype(jnp.bfloat16).reshape(count, D)
    gb_proj = jnp.sum(d_attn.astype(jnp.float32), axis=0)
    d_mixed = times_back(d_attn, w_proj).astype(jnp.bfloat16).reshape(lats, rows, D)
    grad_proj = reduce_scatter(weight_partials(mixed, d_attn, n_cols), by_z, jnp.bfloat16)
    d_mixed_h = to_heads(d_mixed)[0]
    d_qkv = to_tokens(attend_back(query, keys, vals, d_mixed_h, logsum)).reshape(count, 3 * D)
    gb_qkv = jnp.sum(d_qkv.astype(jnp.float32), axis=0)
    gb_qv = jnp.concatenate([gb_qkv[:D], gb_qkv[2 * D :]])
    grad_qkv = reduce_scatter(weight_partials(first, d_qkv, n_cols), by_x, jnp.bfloat16)
    d_first = times_back(d_qkv, w_qkv).reshape(lats, rows, D)
    d_shift1 = jnp.sum(d_first, axis=1)
    d_scale1 = jnp.sum(d_first * norm1, axis=1)
    norm_back1 = jax.vjp(layer_norm, tokens)[1]
    grad_latents = d_middle + norm_back1(d_first * (1.0 + scale1))[0]

    d_modul = jnp.concatenate([d_shift1, d_scale1, d_gate1, d_shift2, d_scale2, d_gate2], axis=1)
    for stride in strides_of(n_cols):
        d_modul = d_modul + swap(d_modul, "seq", stride)
    d_modul = d_modul.astype(jnp.bfloat16)
    modul_cols = small_gather(
        lax.dynamic_slice_in_dim(d_modul, me_col * ada_c, ada_c, 1), "dp"
    )
    grad_ada = cross(acts_rows, modul_cols)
    d_acts = against(modul_cols, ada_block)
    for stride in strides_of(n_cols):
        d_acts = d_acts + swap(d_acts, "seq", stride)
    d_acts = small_gather(d_acts[None], "dp")
    d_act = lax.dynamic_slice_in_dim(d_acts, me_row * lats, lats, 1)
    d_act = d_act.transpose(1, 0, 2).reshape(lats, D)
    silu_back = jax.vjp(jax.nn.silu, condition.astype(jnp.float32))[1]
    grad_condition = silu_back(d_act)[0]

    owner = (me_col == 0).astype(jnp.float32)
    gb_ada = jnp.sum(d_modul.astype(jnp.float32), axis=0) * owner
    bias_all = jnp.concatenate([gb_ada, gb_qv, gb_proj, gb_up, gb_down])
    bias_all = bias_all.reshape(n_rows, n_cols, share)
    bias_sum = reduce_scatter([bias_all[:, j] for j in range(n_cols)], by_z, jnp.float32)
    return (
        output,
        grad_latents,
        grad_condition,
        grad_ada.reshape(-1),
        grad_qkv.astype(jnp.float32).reshape(-1),
        grad_proj.astype(jnp.float32).reshape(-1),
        grad_up.astype(jnp.float32).reshape(-1),
        grad_down.astype(jnp.float32).reshape(-1),
        bias_sum.reshape(-1),
    )


def solution(mesh):
    return jax.shard_map(
        body,
        mesh=mesh,
        in_specs=(
            P("dp", "seq", None),
            P("dp", None),
            P("dp", "seq", None),
            P(("dp", "seq")),
            P(("dp", "seq")),
            P(("dp", "seq")),
            P(("dp", "seq")),
            P(("dp", "seq")),
            P(("dp", "seq")),
        ),
        out_specs=(
            P("dp", "seq", None),
            P("dp", "seq", None),
            P("dp", None),
            P(("dp", "seq")),
            P(("dp", "seq")),
            P(("dp", "seq")),
            P(("dp", "seq")),
            P(("dp", "seq")),
            P(("dp", "seq")),
        ),
        check_vma=False,
    )
```

time: 1550 us -> 1040 us (0.67)
  blocking collectives: 252 us -> 0 us
  local copies, waits for them, and re-layouts: 336 us -> 118 us
  other arithmetic: 273 us -> 131 us
  waiting for transfers between devices: 392 us -> 518 us
  matrix products: 261 us -> 193 us
  starting transfers between devices: 10.3 us -> 52.7 us
    ppermute x0 -> x61, waiting for transfers between devices: none -> 380 us  [the longest x57 322 us: swap(): return lax.ppermute(values, axis, [(d, d ^ stride) for d in range(size)])]
    all_gather x2 -> x0, other arithmetic: 227 us -> none  [the longest x1 167 us: body(): lax.all_gather(qkv_w, ('dp', 'seq'), axis=0, tiled=True)]
    reduce_scatter x3 -> x0, waiting for transfers between devices: 170 us -> none  [the longest x1 84.2 us: body(): lax.psum_scatter(partials[4].astype(jnp.bfloat16), 'dp', scatter_dimensio...]
    transpose x5 -> x0, local copies, waits for them, and re-layouts: 136 us -> none  [blocked(): return flat.reshape(n_rows, n_cols, height // n_rows, breadth // n_cols)....]
    reshape x13 -> x14, local copies, waits for them, and re-layouts: 143 us -> 16 us  [the longest x4 6.77 us: gathered(): block = flat.reshape(1, height // n_rows, breadth // n_cols)]
    all_to_all x2 -> x0, blocking collectives: 121 us -> none  [the longest x1 108 us: body(): lax.all_to_all(d_upper, 'seq', split_axis=1, concat_axis=0, tiled=True)]
    unnamed x20 -> x4, waiting for transfers between devices: 104 us -> 0.07 us
    unnamed x2 -> x0, blocking collectives: 84.5 us -> none
  transfers between devices with their start and end apart: 20 -> 65, of which waited for: 6 -> 39; matrix products, arithmetic and copies ran while one was open for 55% -> 33% of each run, Pallas kernels for 0% -> 0%
where the time goes in v1:
time: 1040 us; the launch traced here: 1030 us
  waiting for transfers between devices  518 us (50%)
  matrix products  193 us (19%)
  other arithmetic  131 us (13%)
  local copies, waits for them, and re-layouts  118 us (11%)
  starting transfers between devices  52.7 us (5%)
  between operations  16.2 us (2%)
    ppermute x57, waiting for transfers between devices, swap(): return lax.ppermute(values, axis, [(d, d ^ stride) for d in range(size)])  322 us
    all_gather x4, waiting for transfers between devices, gathered(): whole = lax.all_gather(block, ('dp', 'seq'), axis=0, tiled=True)  138 us
    ppermute x4, waiting for transfers between devices, shifted(): lax.ppermute(values, 'seq', [(d, (d + shift) % size) for d in range(size)])  57.8 us
    ppermute x57, starting transfers between devices, swap(): return lax.ppermute(values, axis, [(d, d ^ stride) for d in range(size)])  47.3 us
    dot_general x9, matrix products, against(): lax.dot_general(left, right, (((1,), (1,)), ((), ())), preferred_element_...  43.4 us
    dot_general x9, matrix products, cross(): lax.dot_general(left, right, (((0,), (0,)), ((), ())), preferred_element_...  38.6 us
    convert_element_type x6, local copies, waits for them, and re-layouts, weight_partials(): cross(left, right[:, j * width:(j + 1) * width]).astype(jnp.bfloat16)  34.4 us
    convert_element_type x1, other arithmetic, attend_back(): d_scores = (probs * (d_probs - inner)).astype(jnp.bfloat16)  28.5 us
  transfers between devices with their start and end apart: 65, of which 39 were waited for; matrix products, arithmetic and copies ran while one was open for 33% of the time, Pallas kernels for 0%

profile of v1, /device:TPU:0, one launch (start us, length us, event | category | flops | bytes accessed | tf_op | source)
XLA Modules:
  0.0 1027.8 jit_solution(10585628032148963259)
XLA Ops:
  38.2 5.2 collective-permute-done.5
  43.7 6.2 collective-permute-done.6
  59.7 32.7 %all-gather.5.cloned.1.call-done = bf16[32,72,1728]{2,1,0:T(8,128)(2,1)} async-done(((bf16[1,72,1728]{2,1,0:T(8,128)(2,1)}), bf16[32,72,1728]{2,1,0:T(8,128)(2,1)}) %all-gather.5.cloned.1.call-update) | async-done | bytes 7962640 | tf_op jit(solution)/shard_map/all_gather | solution.py:207
  114.1 42.2 %collective-permute-done.10 = bf16[1,512,1728]{1,2,0:T(8,128)(2,1)} collective-permute-done((bf16[1,512,1728]{1,2,0:T(8,128)(2,1)}, bf16[1,512,1728]{1,2,0:T(8,128)(2,1)}, u32[]{:S(2)}, u32[]{:S(2)}) %collective-permute-start.10) | collective-permute-done | bytes 1769504 | tf_op jit(solution)/shard_map/ppermute | solution.py:100
  156.3 7.5 pad_maximum_fusion
  164.2 13.4 %multiply_reduce_fusion.1 = (f32[8,1024]{1,0:T(8,128)S(1)}, f32[8,1024,1024]{1,2,0:T(8,128)}) fusion(bf16[1024,8,72]{0,2,1:T(8,128)(2,1)S(1)} %bitcast.420, bf16[1024,8,72]{0,2,1:T(8,128)(2,1)S(1)} %bitcast.418), kind=kOutput, calls=%fused_computation.6 | convolution fusion | flops 1224728576 | bytes 35946496 | tf_op jit(solution)/shard_map/bqhd,bkhd->bhqk/dot_general | solution.py:157
  177.6 13.7 %fusion = f32[8,1024]{1,0:T(8,128)S(1)} fusion(f32[8,1024,1024]{1,2,0:T(8,128)} %get-tuple-element.95, f32[8,1024]{1,0:T(8,128)S(1)} %get-tuple-element.94), kind=kLoop, calls=%fused_computation.5 | loop fusion | flops 25157632 | bytes 33619968 | tf_op jit(solution)/shard_map/reduce_sum | solution.py:160
  191.4 13.8 %fusion.52 = bf16[8,72,1024]{2,1,0:T(8,128)(2,1)S(1)} fusion(bf16[1024,8,72]{0,2,1:T(8,128)(2,1)S(1)} %bitcast.454, f32[8,1024,1024]{1,2,0:T(8,128)} %get-tuple-element.95, f32[8,1024]{1,0:T(8,128)S(1)} %fusion, f32[8,1024]{1,0:T(8,128)S(1)} %get-tuple-element.94), kind=kOutput, calls=%fused_computation.122 | convolution fusion | flops 1242103808 | bytes 35979264 | tf_op jit(solution)/shard_map/bhqk,bkhd->bqhd/dot_general | solution.py:163
  212.0 15.5 %collective-permute-done.11 = bf16[1,512,576]{1,2,0:T(8,128)(2,1)} collective-permute-done((bf16[1,512,576]{1,2,0:T(8,128)(2,1)S(1)}, bf16[1,512,576]{1,2,0:T(8,128)(2,1)}, u32[]{:S(2)}, u32[]{:S(2)}) %collective-permute-start.11) | collective-permute-done | bytes 589856 | tf_op jit(solution)/shard_map/ppermute | solution.py:100
  234.9 19.1 %all-gather.9.cloned.1.call-done = bf16[32,72,2304]{2,1,0:T(8,128)(2,1)} async-done(((bf16[1,72,2304]{2,1,0:T(8,128)(2,1)}), bf16[32,72,2304]{2,1,0:T(8,128)(2,1)}) %all-gather.9.cloned.1.call-update) | async-done | bytes 10616848 | tf_op jit(solution)/shard_map/all_gather | solution.py:207
  254.0 8.7 fusion.152
  262.7 86.1 %all-gather.11.cloned.1.call-done = bf16[32,288,576]{2,1,0:T(8,128)(2,1)} async-done(((bf16[1,288,576]{2,1,0:T(8,128)(2,1)}), bf16[32,288,576]{2,1,0:T(8,128)(2,1)}) %all-gather.11.cloned.1.call-update) | async-done | bytes 10616848 | tf_op jit(solution)/shard_map/all_gather | solution.py:207
  348.8 5.3 fusion.151
  358.7 5.7 fusion.159
  364.4 6.5 fusion.80
  380.5 16.8 %convert_reduce_fusion = (f32[4608]{0:T(1024)}, bf16[512,4608]{1,0:T(8,128)(2,1)}) fusion(f32[4608]{0:T(1024)S(1)} %copy-done.70, f32[512,2304]{1,0:T(8,128)} %copy-done.39, f32[512,2304]{1,0:T(8,128)} %copy-done.40, f32[512,4608]{1,0:T(8,128)} %fusion.80, bf16[4608,576]{1,0:T(8,128)(2,1)} %bitcast.432, bf16[512,1152]{0,1:T(8,128)(2,1)} %get-tuple-element.49), kind=kOutput, calls=%fused_computation.22 | convolution fusion | flops 2776886784 | bytes 30117888 | tf_op jit(solution)/shard_map/dot_general | solution.py:28
  397.3 5.8 fusion.41
  403.1 6.7 fusion.36
  422.5 5.2 convolution_convert_fusion.1
  427.7 4.6 convolution_convert_fusion
  432.3 4.7 convolution_convert_fusion.3
  448.8 5.3 constant_dynamic-slice_fusion.17
  455.8 8.5 copy.83
  464.3 7.0 convolution_convert_fusion.2
  471.3 23.0 %multiply_reduce_fusion = (f32[8,1024]{1,0:T(8,128)S(1)}, f32[8,1024,1024]{1,2,0:T(8,128)}) fusion(f32[8,1024,1024]{1,2,0:T(8,128)} %get-tuple-element.95, f32[8,1024]{1,0:T(8,128)S(1)} %copy-done.52, bf16[1024,8,72]{0,2,1:T(8,128)(2,1)S(1)} %bitcast.455, bf16[512,8,72]{0,2,1:T(8,128)(2,1)} %bitcast.51, bf16[512,8,72]{0,2,1:T(8,128)(2,1)S(1)} %bitcast.450), kind=kOutput, calls=%fused_computation.1 | convolution fusion | flops 1243865088 | bytes 69533696 | tf_op jit(solution)/shard_map/bqhd,bkhd->bhqk/dot_general | solution.py:174
  494.4 28.5 %multiply_convert_fusion = bf16[8,1024,1024]{1,2,0:T(8,128)(2,1)} fusion(f32[8,1024,1024]{1,2,0:T(8,128)} %get-tuple-element.98, f32[8,1024,1024]{1,2,0:T(8,128)} %get-tuple-element.95, f32[8,1024]{1,0:T(8,128)S(1)} %get-tuple-element.97, f32[8,1024]{1,0:T(8,128)S(1)} %copy-done.52), kind=kLoop, calls=%fused_computation | loop fusion | flops 41943040 | bytes 83951616 | tf_op jit(solution)/shard_map/convert_element_type | solution.py:176
  522.9 11.0 %multiply_convert_fusion.2 = bf16[8,72,1024]{2,1,0:T(8,128)(2,1)S(1)} fusion(bf16[1024,8,72]{0,2,1:T(8,128)(2,1)S(1)} %bitcast.421, bf16[8,1024,1024]{1,2,0:T(8,128)(2,1)} %multiply_convert_fusion), kind=kOutput, calls=%fused_computation.97 | convolution fusion | flops 1209139200 | bytes 19136512 | tf_op jit(solution)/shard_map/bhqk,bqhd->bkhd/dot_general | solution.py:178
  533.9 14.6 %fusion.49 = bf16[8,72,1024]{2,1,0:T(8,128)(2,1)S(1)} fusion(f32[8,1024,1024]{1,2,0:T(8,128)} %get-tuple-element.95, f32[8,1024]{1,0:T(8,128)} %log_add_fusion, bf16[1,512,8,72]{1,3,2,0:T(8,128)(2,1)} %bitcast.61, bf16[1,512,8,72]{1,3,2,0:T(8,128)(2,1)} %bitcast.451), kind=kOutput, calls=%fused_computation.121 | convolution fusion | flops 1236074496 | bytes 35946496 | tf_op jit(solution)/shard_map/bhqk,bqhd->bkhd/dot_general | solution.py:179
  548.4 9.3 multiply_convert_fusion.3
  566.3 23.4 %collective-permute-done.35 = bf16[2,2,72,576]{3,2,1,0:T(8,128)(2,1)S(1)} collective-permute-done((bf16[2,2,72,576]{3,2,1,0:T(8,128)(2,1)S(1)}, bf16[2,2,72,576]{3,2,1,0:T(8,128)(2,1)S(1)}, u32[]{:S(2)}, u32[]{:S(2)}) %collective-permute-start.35) | collective-permute-done | bytes 331808 | tf_op jit(solution)/shard_map/ppermute | solution.py:35
  589.9 7.2 collective-permute-done.31
  614.9 8.4 copy.84
  638.4 4.6 convolution_convert_fusion.5
  653.7 5.8 fusion.35
  660.3 6.5 copy.76
  666.7 6.4 copy.75
  709.2 4.9 collective-permute-done.18
  732.0 55.8 %collective-permute-done.21 = f32[2,16,72]{2,1,0:T(8,128)S(1)} collective-permute-done((f32[2,16,72]{2,1,0:T(8,128)S(1)}, f32[2,16,72]{2,1,0:T(8,128)S(1)}, u32[]{:S(2)}, u32[]{:S(2)}) %collective-permute-start.21) | collective-permute-done | bytes 9248 | tf_op jit(solution)/shard_map/ppermute | solution.py:35
  796.1 6.0 broadcast_select_fusion
  811.6 5.9 broadcast_select_fusion.1
  818.8 78.8 %collective-permute-done.43 = bf16[2,2,72,2304]{3,2,1,0:T(8,128)(2,1)} collective-permute-done((bf16[2,2,72,2304]{3,2,1,0:T(8,128)(2,1)}, bf16[2,2,72,2304]{3,2,1,0:T(8,128)(2,1)}, u32[]{:S(2)}, u32[]{:S(2)}) %collective-permute-start.43) | collective-permute-done | bytes 1327136 | tf_op jit(solution)/shard_map/ppermute | solution.py:35
  903.1 8.1 add_convert_fusion
  914.2 26.6 %collective-permute-done.26 = bf16[2,2,2,72,1728]{4,3,2,1,0:T(8,128)(2,1)} collective-permute-done((bf16[2,2,2,72,1728]{4,3,2,1,0:T(8,128)(2,1)}, bf16[2,2,2,72,1728]{4,3,2,1,0:T(8,128)(2,1)}, u32[]{:S(2)}, u32[]{:S(2)}) %collective-permute-start.26) | collective-permute-done | bytes 1990688 | tf_op jit(solution)/shard_map/ppermute | solution.py:35
  940.8 4.9 add_convert_fusion.1
  951.5 18.2 %collective-permute-done.27 = bf16[2,2,72,1728]{3,2,1,0:T(8,128)(2,1)S(1)} collective-permute-done((bf16[2,2,72,1728]{3,2,1,0:T(8,128)(2,1)S(1)}, bf16[2,2,72,1728]{3,2,1,0:T(8,128)(2,1)S(1)}, u32[]{:S(2)}, u32[]{:S(2)}) %collective-permute-start.27) | collective-permute-done | bytes 995360 | tf_op jit(solution)/shard_map/ppermute | solution.py:35
  974.2 24.1 %collective-permute-done.50 = bf16[2,288,576]{2,1,0:T(8,128)(2,1)} collective-permute-done((bf16[2,288,576]{2,1,0:T(8,128)(2,1)}, bf16[2,288,576]{2,1,0:T(8,128)(2,1)}, u32[]{:S(2)}, u32[]{:S(2)}) %collective-permute-start.50) | collective-permute-done | bytes 663584 | tf_op jit(solution)/shard_map/ppermute | solution.py:35
  999.7 7.0 collective-permute-done.28
  1008.0 6.5 collective-permute-done.51
  (559 shorter events, 270.0 us)
Async XLA Ops:
  7.2 85.3 %all-gather.5.cloned.1.call-start = ((), (), s32[]{:S(2)}) async-start(), calls=%async_computation | async-start | bytes 8515584 | tf_op jit(solution)/shard_map/all_gather | solution.py:207
  9.3 199.9 %all-gather.7.cloned.1.call-start = ((), (), s32[]{:S(2)}) async-start(), calls=%async_computation.1 | async-start | bytes 3041280 | tf_op jit(solution)/shard_map/all_gather | solution.py:207
  11.0 243.0 %all-gather.9.cloned.1.call-start = ((), (), s32[]{:S(2)}) async-start(), calls=%async_computation.2 | async-start | bytes 10948608 | tf_op jit(solution)/shard_map/all_gather | solution.py:207
  13.1 335.6 %all-gather.11.cloned.1.call-start = ((), (), s32[]{:S(2)}) async-start(), calls=%async_computation.3 | async-start | bytes 12165120 | tf_op jit(solution)/shard_map/all_gather | solution.py:207
  14.7 4.6 collective-permute-start
  28.4 8.0 collective-permute-start.4
  37.0 6.4 collective-permute-start.5
  43.5 6.3 collective-permute-start.6
  107.3 49.0 %collective-permute-start.10 = (bf16[1,512,1728]{1,2,0:T(8,128)(2,1)}, bf16[1,512,1728]{1,2,0:T(8,128)(2,1)}, u32[]{:S(2)}, u32[]{:S(2)}) collective-permute-start(bf16[1,512,1728]{1,2,0:T(8,128)(2,1)} %pad_maximum_fusion.3), channel_id=1, source_target_pairs={{0,1},{1,0},{2,3},{3,2},{4,5},{5,4},{6,7},{7,6},{8,9},{9,8},{10,11... | collective-permute-start | bytes 5308424 | tf_op jit(solution)/shard_map/ppermute | solution.py:100
  205.4 22.1 %collective-permute-start.11 = (bf16[1,512,576]{1,2,0:T(8,128)(2,1)S(1)}, bf16[1,512,576]{1,2,0:T(8,128)(2,1)}, u32[]{:S(2)}, u32[]{:S(2)}) collective-permute-start(bf16[1,512,576]{1,2,0:T(8,128)(2,1)S(1)} %get-tuple-element.87), channel_id=1, source_target_pairs={{0,1},{1,0},{2,3},{3,2},{4,5},{5,4},{6,7},{7,6},{8,9},{9,8},{10,11... | collective-permute-start | bytes 1769480 | tf_op jit(solution)/shard_map/ppermute | solution.py:100
  440.2 31.2 %collective-permute-start.12 = (bf16[1,512,576]{1,2,0:T(8,128)(2,1)}, bf16[1,512,576]{1,2,0:T(8,128)(2,1)}, u32[]{:S(2)}, u32[]{:S(2)}) collective-permute-start(bf16[1,512,576]{1,2,0:T(8,128)(2,1)} %bitcast.50), channel_id=1, source_target_pairs={{0,1},{1,0},{2,3},{3,2},{4,5},{5,4},{6,7},{7,6},{8,9},{9,8},{10,11... | collective-permute-start | bytes 1769480 | tf_op jit(solution)/shard_map/ppermute | solution.py:100
  448.3 111.7 %collective-permute-start.34 = (bf16[2,2,2,72,576]{4,3,2,1,0:T(8,128)(2,1)}, bf16[2,2,2,72,576]{4,3,2,1,0:T(8,128)(2,1)}, u32[]{:S(2)}, u32[]{:S(2)}) collective-permute-start(bf16[2,2,2,72,576]{4,3,2,1,0:T(8,128)(2,1)} %dynamic-slice_bitcast_fusion.10), channel_id=1, source_target_pairs={{0,2},{2,0},{4,6},{6,4},{8,10},{10,8},{12,14},{14,12},{16,18},{18,... | collective-permute-start | bytes 1990664 | tf_op jit(solution)/shard_map/ppermute | solution.py:35
  448.3 115.3 %collective-permute-start.30 = (bf16[2,2,2,72,576]{4,3,2,1,0:T(8,128)(2,1)}, bf16[2,2,2,72,576]{4,3,2,1,0:T(8,128)(2,1)}, u32[]{:S(2)}, u32[]{:S(2)}) collective-permute-start(bf16[2,2,2,72,576]{4,3,2,1,0:T(8,128)(2,1)} %dynamic-slice_bitcast_fusion.11), channel_id=1, source_target_pairs={{0,2},{2,0},{4,6},{6,4},{8,10},{10,8},{12,14},{14,12},{16,18},{18,... | collective-permute-start | bytes 1990664 | tf_op jit(solution)/shard_map/ppermute | solution.py:35
  559.3 71.6 %collective-permute-start.13 = (bf16[1,512,1728]{1,2,0:T(8,128)(2,1)}, bf16[1,512,1728]{1,2,0:T(8,128)(2,1)}, u32[]{:S(2)}, u32[]{:S(2)}) collective-permute-start(bf16[1,512,1728]{1,2,0:T(8,128)(2,1)} %pad_maximum_fusion.1), channel_id=1, source_target_pairs={{0,1},{1,0},{2,3},{3,2},{4,5},{5,4},{6,7},{7,6},{8,9},{9,8},{10,11... | collective-permute-start | bytes 5308424 | tf_op jit(solution)/shard_map/ppermute | solution.py:100
  561.9 27.8 %collective-permute-start.35 = (bf16[2,2,72,576]{3,2,1,0:T(8,128)(2,1)S(1)}, bf16[2,2,72,576]{3,2,1,0:T(8,128)(2,1)S(1)}, u32[]{:S(2)}, u32[]{:S(2)}) collective-permute-start(bf16[2,2,72,576]{3,2,1,0:T(8,128)(2,1)S(1)} %dynamic-slice_bitcast_fusion.21), channel_id=1, source_target_pairs={{0,16},{2,18},{4,20},{6,22},{8,24},{10,26},{12,28},{14,30},{16,0},... | collective-permute-start | bytes 995336 | tf_op jit(solution)/shard_map/ppermute | solution.py:35
  564.9 32.2 %collective-permute-start.31 = (bf16[2,2,72,576]{3,2,1,0:T(8,128)(2,1)S(1)}, bf16[2,2,72,576]{3,2,1,0:T(8,128)(2,1)S(1)}, u32[]{:S(2)}, u32[]{:S(2)}) collective-permute-start(bf16[2,2,72,576]{3,2,1,0:T(8,128)(2,1)S(1)} %dynamic-slice_bitcast_fusion.22), channel_id=1, source_target_pairs={{0,16},{2,18},{4,20},{6,22},{8,24},{10,26},{12,28},{14,30},{16,0},... | collective-permute-start | bytes 995336 | tf_op jit(solution)/shard_map/ppermute | solution.py:35
  589.8 11.2 %collective-permute-start.36 = (bf16[2,72,576]{2,1,0:T(8,128)(2,1)S(1)}, bf16[2,72,576]{2,1,0:T(8,128)(2,1)S(1)}, u32[]{:S(2)}, u32[]{:S(2)}) collective-permute-start(bf16[2,72,576]{2,1,0:T(8,128)(2,1)S(1)} %dynamic-slice_bitcast_fusion.25), channel_id=1, source_target_pairs={{0,8},{2,10},{4,12},{6,14},{8,0},{10,2},{12,4},{14,6},{16,24},{18,... | collective-permute-start | bytes 497672 | tf_op jit(solution)/shard_map/ppermute | solution.py:35
  597.2 7.7 collective-permute-start.32
  601.1 22.2 %collective-permute-start.37 = (bf16[72,576]{1,0:T(8,128)(2,1)S(1)}, bf16[72,576]{1,0:T(8,128)(2,1)S(1)}, u32[]{:S(2)}, u32[]{:S(2)}) collective-permute-start(bf16[72,576]{1,0:T(8,128)(2,1)S(1)} %dynamic-slice_bitcast_fusion.28), channel_id=1, source_target_pairs={{0,4},{2,6},{4,0},{6,2},{8,12},{10,14},{12,8},{14,10},{16,20},{18,... | collective-permute-start | bytes 248840 | tf_op jit(solution)/shard_map/ppermute | solution.py:35
  605.0 18.3 %collective-permute-start.33 = (bf16[72,576]{1,0:T(8,128)(2,1)S(1)}, bf16[72,576]{1,0:T(8,128)(2,1)S(1)}, u32[]{:S(2)}, u32[]{:S(2)}) collective-permute-start(bf16[72,576]{1,0:T(8,128)(2,1)S(1)} %dynamic-slice_bitcast_fusion.29), channel_id=1, source_target_pairs={{0,4},{2,6},{4,0},{6,2},{8,12},{10,14},{12,8},{14,10},{16,20},{18,... | collective-permute-start | bytes 248840 | tf_op jit(solution)/shard_map/ppermute | solution.py:35
  614.4 105.0 %collective-permute-start.39 = (bf16[2,2,2,72,2304]{4,3,2,1,0:T(8,128)(2,1)}, bf16[2,2,2,72,2304]{4,3,2,1,0:T(8,128)(2,1)}, u32[]{:S(2)}, u32[]{:S(2)}) collective-permute-start(bf16[2,2,2,72,2304]{4,3,2,1,0:T(8,128)(2,1)} %dynamic-slice_bitcast_fusion.2), channel_id=1, source_target_pairs={{0,2},{2,0},{4,6},{6,4},{8,10},{10,8},{12,14},{14,12},{16,18},{18,... | collective-permute-start | bytes 7962632 | tf_op jit(solution)/shard_map/ppermute | solution.py:35
  614.4 109.1 %collective-permute-start.41 = (bf16[2,2,2,72,2304]{4,3,1,0,2:T(8,128)(2,1)}, bf16[2,2,2,72,2304]{4,3,1,0,2:T(8,128)(2,1)}, u32[]{:S(2)}, u32[]{:S(2)}) collective-permute-start(bf16[2,2,2,72,2304]{4,3,1,0,2:T(8,128)(2,1)} %bitcast.396), channel_id=1, source_target_pairs={{0,2},{2,0},{4,6},{6,4},{8,10},{10,8},{12,14},{14,12},{16,18},{18,... | collective-permute-start | bytes 7962632 | tf_op jit(solution)/shard_map/ppermute | solution.py:35
  623.4 6.6 collective-permute-start.38
  628.7 166.6 %collective-permute-start.47 = (bf16[2,2,2,288,576]{4,3,2,1,0:T(8,128)(2,1)}, bf16[2,2,2,288,576]{4,3,2,1,0:T(8,128)(2,1)}, u32[]{:S(2)}, u32[]{:S(2)}) collective-permute-start(bf16[2,2,2,288,576]{4,3,2,1,0:T(8,128)(2,1)} %dynamic-slice_bitcast_fusion), channel_id=1, source_target_pairs={{0,2},{2,0},{4,6},{6,4},{8,10},{10,8},{12,14},{14,12},{16,18},{18,... | collective-permute-start | bytes 7962632 | tf_op jit(solution)/shard_map/ppermute | solution.py:35
  630.0 165.9 %collective-permute-start.46 = (bf16[2,2,2,288,576]{4,3,2,1,0:T(8,128)(2,1)}, bf16[2,2,2,288,576]{4,3,2,1,0:T(8,128)(2,1)}, u32[]{:S(2)}, u32[]{:S(2)}) collective-permute-start(bf16[2,2,2,288,576]{4,3,2,1,0:T(8,128)(2,1)} %dynamic-slice_bitcast_fusion.1), channel_id=1, source_target_pairs={{0,2},{2,0},{4,6},{6,4},{8,10},{10,8},{12,14},{14,12},{16,18},{18,... | collective-permute-start | bytes 7962632 | tf_op jit(solution)/shard_map/ppermute | solution.py:35
  659.5 21.4 %collective-permute-start.14 = (f32[1,6912]{1,0:T(1,128)S(1)}, f32[1,6912]{1,0:T(1,128)S(1)}, u32[]{:S(2)}, u32[]{:S(2)}) collective-permute-start(f32[1,6912]{1,0:T(1,128)S(1)} %constant_dynamic-update-slice_fusion), channel_id=1, source_target_pairs={{0,1},{1,0},{2,3},{3,2},{4,5},{5,4},{6,7},{7,6},{8,9},{9,8},{10,11... | collective-permute-start | bytes 82952 | tf_op jit(solution)/shard_map/ppermute | solution.py:35
  688.7 4.5 collective-permute-start.53
  709.0 5.2 collective-permute-start.18
  718.0 10.6 %collective-permute-start.55 = (f32[1,504]{1,0:T(1,128)S(1)}, f32[1,504]{1,0:T(1,128)S(1)}, u32[]{:S(2)}, u32[]{:S(2)}) collective-permute-start(f32[1,504]{1,0:T(1,128)S(1)} %fusion.129), channel_id=1, source_target_pairs={{0,4},{2,6},{4,0},{6,2},{8,12},{10,14},{12,8},{14,10},{16,20},{18,... | collective-permute-start | bytes 6056 | tf_op jit(solution)/shard_map/ppermute | solution.py:35
  719.4 11.3 %collective-permute-start.59 = (f32[1,504]{1,0:T(1,128)S(1)}, f32[1,504]{1,0:T(1,128)S(1)}, u32[]{:S(2)}, u32[]{:S(2)}) collective-permute-start(f32[1,504]{1,0:T(1,128)S(1)} %fusion.132), channel_id=1, source_target_pairs={{0,4},{2,6},{4,0},{6,2},{8,12},{10,14},{12,8},{14,10},{16,20},{18,... | collective-permute-start | bytes 6056 | tf_op jit(solution)/shard_map/ppermute | solution.py:35
  723.5 6.4 collective-permute-start.20
  728.6 73.5 %collective-permute-start.40 = (bf16[2,2,72,2304]{3,2,1,0:T(8,128)(2,1)S(1)}, bf16[2,2,72,2304]{3,2,1,0:T(8,128)(2,1)S(1)}, u32[]{:S(2)}, u32[]{:S(2)}) collective-permute-start(bf16[2,2,72,2304]{3,2,1,0:T(8,128)(2,1)S(1)} %dynamic-slice_bitcast_fusion.7), channel_id=1, source_target_pairs={{0,4},{2,6},{4,0},{6,2},{8,12},{10,14},{12,8},{14,10},{16,20},{18,... | collective-permute-start | bytes 3981320 | tf_op jit(solution)/shard_map/ppermute | solution.py:35
  729.9 73.5 %collective-permute-start.42 = (bf16[2,2,72,2304]{3,2,1,0:T(8,128)(2,1)}, bf16[2,2,72,2304]{3,2,1,0:T(8,128)(2,1)}, u32[]{:S(2)}, u32[]{:S(2)}) collective-permute-start(bf16[2,2,72,2304]{3,2,1,0:T(8,128)(2,1)} %dynamic-slice_bitcast_fusion.6), channel_id=1, source_target_pairs={{0,4},{2,6},{4,0},{6,2},{8,12},{10,14},{12,8},{14,10},{16,20},{18,... | collective-permute-start | bytes 3981320 | tf_op jit(solution)/shard_map/ppermute | solution.py:35
  730.6 57.2 %collective-permute-start.21 = (f32[2,16,72]{2,1,0:T(8,128)S(1)}, f32[2,16,72]{2,1,0:T(8,128)S(1)}, u32[]{:S(2)}, u32[]{:S(2)}) collective-permute-start(f32[2,16,72]{2,1,0:T(8,128)S(1)} %maximum_select_fusion.14), channel_id=1, source_target_pairs={{0,4},{2,6},{4,0},{6,2},{8,12},{10,14},{12,8},{14,10},{16,20},{18,... | collective-permute-start | bytes 27656 | tf_op jit(solution)/shard_map/ppermute | solution.py:35
  795.3 16.3 %collective-permute-start.25 = (bf16[2,2,2,72,1728]{4,3,2,1,0:T(8,128)(2,1)}, bf16[2,2,2,72,1728]{4,3,2,1,0:T(8,128)(2,1)}, u32[]{:S(2)}, u32[]{:S(2)}) collective-permute-start(bf16[2,2,2,72,1728]{4,3,2,1,0:T(8,128)(2,1)} %dynamic-slice_bitcast_fusion.3), channel_id=1, source_target_pairs={{0,2},{2,0},{4,6},{6,4},{8,10},{10,8},{12,14},{14,12},{16,18},{18,... | collective-permute-start | bytes 5971976 | tf_op jit(solution)/shard_map/ppermute | solution.py:35
  795.3 16.3 %collective-permute-start.24 = (bf16[2,2,2,72,1728]{4,3,2,1,0:T(8,128)(2,1)}, bf16[2,2,2,72,1728]{4,3,2,1,0:T(8,128)(2,1)}, u32[]{:S(2)}, u32[]{:S(2)}) collective-permute-start(bf16[2,2,2,72,1728]{4,3,2,1,0:T(8,128)(2,1)} %dynamic-slice_bitcast_fusion.4), channel_id=1, source_target_pairs={{0,2},{2,0},{4,6},{6,4},{8,10},{10,8},{12,14},{14,12},{16,18},{18,... | collective-permute-start | bytes 5971976 | tf_op jit(solution)/shard_map/ppermute | solution.py:35
  795.9 14.9 %collective-permute-start.23 = (f32[8,16,72]{2,1,0:T(8,128)S(1)}, f32[8,16,72]{2,1,0:T(8,128)S(1)}, u32[]{:S(2)}, u32[]{:S(2)}) collective-permute-start(f32[8,16,72]{2,1,0:T(8,128)S(1)} %maximum_select_fusion.6), channel_id=1, source_target_pairs={{0,16},{2,18},{4,20},{6,22},{8,24},{10,26},{12,28},{14,30},{16,0},... | collective-permute-start | bytes 110600 | tf_op jit(solution)/shard_map/ppermute | solution.py:35
  802.1 101.0 %collective-permute-start.48 = (bf16[2,2,2,288,576]{4,3,2,1,0:T(8,128)(2,1)}, bf16[2,2,2,288,576]{4,3,2,1,0:T(8,128)(2,1)}, u32[]{:S(2)}, u32[]{:S(2)}) collective-permute-start(bf16[2,2,2,288,576]{4,3,2,1,0:T(8,128)(2,1)} %broadcast_select_fusion), channel_id=1, source_target_pairs={{0,1},{1,0},{2,3},{3,2},{4,5},{5,4},{6,7},{7,6},{8,9},{9,8},{10,11... | collective-permute-start | bytes 7962632 | tf_op jit(solution)/shard_map/ppermute | solution.py:35
  806.6 91.0 %collective-permute-start.43 = (bf16[2,2,72,2304]{3,2,1,0:T(8,128)(2,1)}, bf16[2,2,72,2304]{3,2,1,0:T(8,128)(2,1)}, u32[]{:S(2)}, u32[]{:S(2)}) collective-permute-start(bf16[2,2,72,2304]{3,2,1,0:T(8,128)(2,1)} %broadcast_select_fusion.2), channel_id=1, source_target_pairs={{0,1},{1,0},{2,3},{3,2},{4,5},{5,4},{6,7},{7,6},{8,9},{9,8},{10,11... | collective-permute-start | bytes 3981320 | tf_op jit(solution)/shard_map/ppermute | solution.py:35
  817.5 123.3 %collective-permute-start.26 = (bf16[2,2,2,72,1728]{4,3,2,1,0:T(8,128)(2,1)}, bf16[2,2,2,72,1728]{4,3,2,1,0:T(8,128)(2,1)}, u32[]{:S(2)}, u32[]{:S(2)}) collective-permute-start(bf16[2,2,2,72,1728]{4,3,2,1,0:T(8,128)(2,1)} %broadcast_select_fusion.1), channel_id=1, source_target_pairs={{0,1},{1,0},{2,3},{3,2},{4,5},{5,4},{6,7},{7,6},{8,9},{9,8},{10,11... | collective-permute-start | bytes 5971976 | tf_op jit(solution)/shard_map/ppermute | solution.py:35
  900.2 47.0 %collective-permute-start.44 = (bf16[2,72,2304]{2,1,0:T(8,128)(2,1)S(1)}, bf16[2,72,2304]{2,1,0:T(8,128)(2,1)S(1)}, u32[]{:S(2)}, u32[]{:S(2)}) collective-permute-start(bf16[2,72,2304]{2,1,0:T(8,128)(2,1)S(1)} %dynamic-slice_bitcast_fusion.12), channel_id=1, source_target_pairs={{0,16},{2,18},{4,20},{6,22},{8,24},{10,26},{12,28},{14,30},{16,0},... | collective-permute-start | bytes 1990664 | tf_op jit(solution)/shard_map/ppermute | solution.py:35
  912.7 36.6 %collective-permute-start.49 = (bf16[2,2,288,576]{3,2,1,0:T(8,128)(2,1)S(1)}, bf16[2,2,288,576]{3,2,1,0:T(8,128)(2,1)S(1)}, u32[]{:S(2)}, u32[]{:S(2)}) collective-permute-start(bf16[2,2,288,576]{3,2,1,0:T(8,128)(2,1)S(1)} %dynamic-slice_bitcast_fusion.5), channel_id=1, source_target_pairs={{0,4},{2,6},{4,0},{6,2},{8,12},{10,14},{12,8},{14,10},{16,20},{18,... | collective-permute-start | bytes 3981320 | tf_op jit(solution)/shard_map/ppermute | solution.py:35
  945.8 23.9 %collective-permute-start.27 = (bf16[2,2,72,1728]{3,2,1,0:T(8,128)(2,1)S(1)}, bf16[2,2,72,1728]{3,2,1,0:T(8,128)(2,1)S(1)}, u32[]{:S(2)}, u32[]{:S(2)}) collective-permute-start(bf16[2,2,72,1728]{3,2,1,0:T(8,128)(2,1)S(1)} %dynamic-slice_bitcast_fusion.8), channel_id=1, source_target_pairs={{0,4},{2,6},{4,0},{6,2},{8,12},{10,14},{12,8},{14,10},{16,20},{18,... | collective-permute-start | bytes 2985992 | tf_op jit(solution)/shard_map/ppermute | solution.py:35
  947.4 25.8 %collective-permute-start.45 = (bf16[72,2304]{1,0:T(8,128)(2,1)S(1)}, bf16[72,2304]{1,0:T(8,128)(2,1)S(1)}, u32[]{:S(2)}, u32[]{:S(2)}) collective-permute-start(bf16[72,2304]{1,0:T(8,128)(2,1)S(1)} %dynamic-slice_bitcast_fusion.23), channel_id=1, source_target_pairs={{0,8},{2,10},{4,12},{6,14},{8,0},{10,2},{12,4},{14,6},{16,24},{18,... | collective-permute-start | bytes 995336 | tf_op jit(solution)/shard_map/ppermute | solution.py:35
  950.7 47.6 %collective-permute-start.50 = (bf16[2,288,576]{2,1,0:T(8,128)(2,1)}, bf16[2,288,576]{2,1,0:T(8,128)(2,1)}, u32[]{:S(2)}, u32[]{:S(2)}) collective-permute-start(bf16[2,288,576]{2,1,0:T(8,128)(2,1)} %dynamic-slice_bitcast_fusion.9), channel_id=1, source_target_pairs={{0,16},{2,18},{4,20},{6,22},{8,24},{10,26},{12,28},{14,30},{16,0},... | collective-permute-start | bytes 1990664 | tf_op jit(solution)/shard_map/ppermute | solution.py:35
  970.8 36.0 %collective-permute-start.28 = (bf16[2,72,1728]{2,1,0:T(8,128)(2,1)}, bf16[2,72,1728]{2,1,0:T(8,128)(2,1)}, u32[]{:S(2)}, u32[]{:S(2)}) collective-permute-start(bf16[2,72,1728]{2,1,0:T(8,128)(2,1)} %dynamic-slice_bitcast_fusion.19), channel_id=1, source_target_pairs={{0,16},{2,18},{4,20},{6,22},{8,24},{10,26},{12,28},{14,30},{16,0},... | collective-permute-start | bytes 1493000 | tf_op jit(solution)/shard_map/ppermute | solution.py:35
  999.6 14.9 %collective-permute-start.51 = (bf16[288,576]{1,0:T(8,128)(2,1)S(1)}, bf16[288,576]{1,0:T(8,128)(2,1)S(1)}, u32[]{:S(2)}, u32[]{:S(2)}) collective-permute-start(bf16[288,576]{1,0:T(8,128)(2,1)S(1)} %dynamic-slice_bitcast_fusion.20), channel_id=1, source_target_pairs={{0,8},{2,10},{4,12},{6,14},{8,0},{10,2},{12,4},{14,6},{16,24},{18,... | collective-permute-start | bytes 995336 | tf_op jit(solution)/shard_map/ppermute | solution.py:35
  1007.9 12.0 %collective-permute-start.29 = (bf16[72,1728]{1,0:T(8,128)(2,1)S(1)}, bf16[72,1728]{1,0:T(8,128)(2,1)S(1)}, u32[]{:S(2)}, u32[]{:S(2)}) collective-permute-start(bf16[72,1728]{1,0:T(8,128)(2,1)S(1)} %dynamic-slice_bitcast_fusion.24), channel_id=1, source_target_pairs={{0,8},{2,10},{4,12},{6,14},{8,0},{10,2},{12,4},{14,6},{16,24},{18,... | collective-permute-start | bytes 746504 | tf_op jit(solution)/shard_map/ppermute | solution.py:35
  (139 other events, 2676.7 us)
Sparse Core Ops, SparseCore 0:
  11.5 80.8 all-gather.4
  95.9 63.3 all-gather.6
  162.8 91.1 all-gather.8
  257.4 91.3 all-gather.10

commit v2 on v1

--- a/solution.py
+++ b/solution.py
@@ -61,28 +61,52 @@
     return (keep.astype(jnp.float32) + got.astype(jnp.float32)).astype(wire)
 
 
+class Scatter:
+    def __init__(self, columns, order, wire):
+        n_rows = lax.axis_size("dp")
+        self.axis_of = strides_of(n_rows)[::-1]
+        height, width = columns[0].shape
+        shape = (2,) * len(self.axis_of) + (height // n_rows, width)
+        self.state = [c.reshape(shape) for c in columns]
+        self.order = list(order)
+        self.wire = wire
+
+    def step(self):
+        if not self.order:
+            return self
+        axis, stride = self.order.pop(0)
+        if axis == "dp":
+            self.state = [halve_rows(s, self.axis_of, stride, self.wire) for s in self.state]
+            self.axis_of = [s for s in self.axis_of if s != stride]
+            return self
+        half = len(self.state) // 2
+        high = ((lax.axis_index("seq") // half) % 2) == 1
+        nxt = []
+        for a, b in zip(self.state[:half], self.state[half:]):
+            send = jnp.where(high, a, b)
+            keep = jnp.where(high, b, a)
+            got = swap(send.astype(self.wire), "seq", half)
+            total = keep.astype(jnp.float32) + got.astype(jnp.float32)
+            nxt.append(total.astype(self.wire))
+        self.state = nxt
+        return self
+
+    def result(self):
+        while self.order:
+            self.step()
+        return self.state[0]
+
+
 def reduce_scatter(columns, order, wire):
-    n_rows = lax.axis_size("dp")
-    axis_of = strides_of(n_rows)[::-1]
-    height, width = columns[0].shape
-    shape = (2,) * len(axis_of) + (height // n_rows, width)
-    state = [c.reshape(shape) for c in columns]
-    me_col = lax.axis_index("seq")
-    for axis, stride in order:
-        if axis == "dp":
-            state = [halve_rows(s, axis_of, stride, wire) for s in state]
-            axis_of = [s for s in axis_of if s != stride]
-        else:
-            half = len(state) // 2
-            high = ((me_col // half) % 2) == 1
-            nxt = []
-            for a, b in zip(state[:half], state[half:]):
-                send = jnp.where(high, a, b)
-                keep = jnp.where(high, b, a)
-                got = swap(send.astype(wire), "seq", half)
-                nxt.append((keep.astype(jnp.float32) + got.astype(jnp.float32)).astype(wire))
-            state = nxt
-    return state[0]
+    return Scatter(columns, order, wire).result()
+
+
+def tie(value, *scatters):
+    held = [s.state for s in scatters]
+    value, held = lax.optimization_barrier((value, held))
+    for s, state in zip(scatters, held):
+        s.state = state
+    return value
 
 
 def orders():
@@ -164,7 +188,7 @@
     return mixed.astype(jnp.bfloat16).reshape(lats, total, wide), logsum
 
 
-def attend_back(query, keys, vals, d_mixed, logsum):
+def attend_back(query, keys, vals, d_mixed, logsum, down, up, proj):
     lats, total, wide = query.shape
     heads = wide // HD
     scale = HD ** (-0.5)
@@ -173,12 +197,16 @@
     probs = jnp.exp(again - logsum)
     d_probs = jnp.einsum("bqhd,bkhd->bhqk", d, v, preferred_element_type=jnp.float32)
     inner = jnp.sum(d_probs * probs, axis=-1, keepdims=True)
+    inner = tie(inner, proj.step())
     d_scores = (probs * (d_probs - inner)).astype(jnp.bfloat16)
-    dq = jnp.einsum("bhqk,bkhd->bqhd", d_scores, k, preferred_element_type=jnp.float32) * scale
-    dk = jnp.einsum("bhqk,bqhd->bkhd", d_scores, q, preferred_element_type=jnp.float32) * scale
+    d_scores = tie(d_scores, down.step())
     dv = jnp.einsum(
         "bhqk,bqhd->bkhd", probs.astype(jnp.bfloat16), d, preferred_element_type=jnp.float32
     )
+    dv, d_scores = tie((dv, d_scores), up.step(), proj.step())
+    dk = jnp.einsum("bhqk,bqhd->bkhd", d_scores, q, preferred_element_type=jnp.float32) * scale
+    dk, d_scores = tie((dk, d_scores), down.step(), proj.step())
+    dq = jnp.einsum("bhqk,bkhd->bqhd", d_scores, k, preferred_element_type=jnp.float32) * scale
     return [a.astype(jnp.bfloat16).reshape(lats, total, wide) for a in (dq, dk, dv)]
 
 
@@ -201,12 +229,10 @@
     ]
 
 
-def gathered(flat, height, breadth):
+def gathered(flat):
     n_rows, n_cols = lax.axis_size("dp"), lax.axis_size("seq")
-    block = flat.reshape(1, height // n_rows, breadth // n_cols)
-    whole = lax.all_gather(block, ("dp", "seq"), axis=0, tiled=True)
-    whole = whole.reshape(n_rows, n_cols, height // n_rows, breadth // n_cols)
-    return [whole[:, j].reshape(height, breadth // n_cols) for j in range(n_cols)]
+    whole = lax.all_gather(flat[None], ("dp", "seq"), axis=0, tiled=True)
+    return whole.reshape((n_rows, n_cols) + flat.shape)
 
 
 def body(latents, condition, cotangent, ada_w, qkv_w, proj_w, fc1_w, fc2_w, biases):
@@ -222,10 +248,22 @@
     payload = small_gather(small_gather(payload, "seq"), "dp")
     b_all = payload[:, :share].reshape(-1).astype(jnp.float32)
     conds = payload[:, share:].reshape(n_rows, n_cols, lats, D)[:, 0].reshape(n_rows * lats, D)
-    w_qkv = gathered(qkv_w, D, 3 * D)
-    w_proj = gathered(proj_w, D, D)
-    w_up = gathered(fc1_w, D, FF)
-    w_down = gathered(fc2_w, FF, D)
+    side, narrow, slabs = D // n_rows, D // n_cols, FF // D
+    whole = gathered(
+        jnp.concatenate([qkv_w.reshape(side, 3 * narrow), proj_w.reshape(side, narrow)], axis=1)
+    )
+    w_qkv = [whole[:, j, :, : 3 * narrow].reshape(D, 3 * narrow) for j in range(n_cols)]
+    w_proj = [whole[:, j, :, 3 * narrow :].reshape(D, narrow) for j in range(n_cols)]
+    fc2_wide = fc2_w.reshape(slabs, side, narrow)
+    fc2_wide = jnp.concatenate([fc2_wide[p] for p in range(slabs)], axis=1)
+    whole = gathered(jnp.stack([fc1_w.reshape(side, slabs * narrow), fc2_wide]))
+    w_up = [whole[:, j, 0].reshape(D, slabs * narrow) for j in range(n_cols)]
+    w_down = [
+        jnp.stack(
+            [whole[:, j, 1, :, p * narrow : (p + 1) * narrow] for p in range(slabs)], axis=1
+        ).reshape(FF, narrow)
+        for j in range(n_cols)
+    ]
     b_ada = b_all[: 6 * D]
     b_qv = b_all[6 * D : 8 * D]
     b_proj = b_all[8 * D : 9 * D]
@@ -265,12 +303,15 @@
     d_gate2 = jnp.sum(grad_out * branch, axis=1)
     d_branch = (gate2 * grad_out).astype(jnp.bfloat16).reshape(count, D)
     gb_down = jnp.sum(d_branch.astype(jnp.float32), axis=0)
-    grad_down = reduce_scatter(weight_partials(hidden, d_branch, n_cols), by_x, jnp.bfloat16)
+    down = Scatter(weight_partials(hidden, d_branch, n_cols), by_y, jnp.bfloat16)
+    d_branch = tie(d_branch, down)
     d_hidden = times_back(d_branch, w_down)
     gelu_back = jax.vjp(gelu_tanh, upper)[1]
     d_upper = gelu_back(d_hidden)[0].astype(jnp.bfloat16)
     gb_up = jnp.sum(d_upper.astype(jnp.float32), axis=0)
-    grad_up = reduce_scatter(weight_partials(second, d_upper, n_cols), by_y, jnp.bfloat16)
+    d_upper = tie(d_upper, down.step())
+    up = Scatter(weight_partials(second, d_upper, n_cols), by_x, jnp.bfloat16)
+    d_upper = tie(d_upper, up)
     d_second = times_back(d_upper, w_up).reshape(lats, rows, D)
     d_shift2 = jnp.sum(d_second, axis=1)
     d_scale2 = jnp.sum(d_second * norm2, axis=1)
@@ -280,13 +321,20 @@
     d_attn = (gate1 * d_middle).astype(jnp.bfloat16).reshape(count, D)
     gb_proj = jnp.sum(d_attn.astype(jnp.float32), axis=0)
     d_mixed = times_back(d_attn, w_proj).astype(jnp.bfloat16).reshape(lats, rows, D)
-    grad_proj = reduce_scatter(weight_partials(mixed, d_attn, n_cols), by_z, jnp.bfloat16)
-    d_mixed_h = to_heads(d_mixed)[0]
-    d_qkv = to_tokens(attend_back(query, keys, vals, d_mixed_h, logsum)).reshape(count, 3 * D)
+    proj = Scatter(weight_partials(mixed, d_attn, n_cols), by_z, jnp.bfloat16)
+    d_mixed_h = tie(to_heads(d_mixed)[0], proj, up.step())
+    d_heads = attend_back(query, keys, vals, d_mixed_h, logsum, down, up, proj)
+    d_qkv = to_tokens(tie(d_heads, up.step(), proj.step())).reshape(count, 3 * D)
+    d_qkv = tie(d_qkv, down.step(), up.step(), proj.step())
     gb_qkv = jnp.sum(d_qkv.astype(jnp.float32), axis=0)
     gb_qv = jnp.concatenate([gb_qkv[:D], gb_qkv[2 * D :]])
-    grad_qkv = reduce_scatter(weight_partials(first, d_qkv, n_cols), by_x, jnp.bfloat16)
+    partials = weight_partials(first, d_qkv, n_cols)
+    cut = partials[0].shape[1] // 256 * 128
+    left = Scatter([p[:, :cut] for p in partials], by_x, jnp.bfloat16)
+    right = Scatter([p[:, cut:] for p in partials], by_y, jnp.bfloat16)
+    d_qkv = tie(d_qkv, left, right)
     d_first = times_back(d_qkv, w_qkv).reshape(lats, rows, D)
+    d_first = tie(d_first, left.step(), right.step(), down.step(), up.step())
     d_shift1 = jnp.sum(d_first, axis=1)
     d_scale1 = jnp.sum(d_first * norm1, axis=1)
     norm_back1 = jax.vjp(layer_norm, tokens)[1]
@@ -299,11 +347,15 @@
     modul_cols = small_gather(
         lax.dynamic_slice_in_dim(d_modul, me_col * ada_c, ada_c, 1), "dp"
     )
+    modul_cols = tie(modul_cols, left.step(), right.step())
     grad_ada = cross(acts_rows, modul_cols)
     d_acts = against(modul_cols, ada_block)
     for stride in strides_of(n_cols):
         d_acts = d_acts + swap(d_acts, "seq", stride)
     d_acts = small_gather(d_acts[None], "dp")
+    d_acts = tie(d_acts, left.step(), right.step())
+    grad_down, grad_up, grad_proj = down.result(), up.result(), proj.result()
+    grad_qkv = jnp.concatenate([left.result(), right.result()], axis=1)
     d_act = lax.dynamic_slice_in_dim(d_acts, me_row * lats, lats, 1)
     d_act = d_act.transpose(1, 0, 2).reshape(lats, D)
     silu_back = jax.vjp(jax.nn.silu, condition.astype(jnp.float32))[1]
@@ -312,8 +364,9 @@
     owner = (me_col == 0).astype(jnp.float32)
     gb_ada = jnp.sum(d_modul.astype(jnp.float32), axis=0) * owner
     bias_all = jnp.concatenate([gb_ada, gb_qv, gb_proj, gb_up, gb_down])
+    bias_order = [("seq", s) for s in strides_of(n_cols)[::-1]] + dp_order
     bias_all = bias_all.reshape(n_rows, n_cols, share)
-    bias_sum = reduce_scatter([bias_all[:, j] for j in range(n_cols)], by_z, jnp.float32)
+    bias_sum = reduce_scatter([bias_all[:, j] for j in range(n_cols)], bias_order, jnp.float32)
     return (
         output,
         grad_latents,

time: 1040 us -> 839 us (0.81)
  waiting for transfers between devices: 518 us -> 290 us
  local copies, waits for them, and re-layouts: 118 us -> 132 us
    ppermute x57 -> x60, waiting for transfers between devices: 322 us -> 171 us  [swap(): return lax.ppermute(values, axis, [(d, d ^ stride) for d in range(size)])]
    all_gather x4 -> x2, waiting for transfers between devices: 138 us -> 51.3 us  [gathered(): whole = lax.all_gather(flat[None], ('dp', 'seq'), axis=0, tiled=True)]
    convert_element_type x13 -> x30, other arithmetic: 13.7 us -> 36.6 us  [halve_rows(): return (keep.astype(jnp.float32) + got.astype(jnp.float32)).astype(wire)]
    slice x5 -> x12, local copies, waits for them, and re-layouts: 19.9 us -> 33.7 us  [the longest x4 10.5 us: body(): left = Scatter([p[:, :cut] for p in partials], by_x, jnp.bfloat16)]
    convert_element_type x6 -> x4, local copies, waits for them, and re-layouts: 34.4 us -> 21.6 us  [weight_partials(): cross(left, right[:, j * width:(j + 1) * width]).astype(jnp.bfloat16)]
    dot_general x9, matrix products: 38.6 us -> 27.5 us  [cross(): lax.dot_general(left, right, (((0,), (0,)), ((), ())), preferred_element_...]
    another operation x3 -> x7, local copies, waits for them, and re-layouts: 1.9 us -> 12.9 us  [the longest x3 7.7 us: body(): jnp.stack([whole[:, j, 1, :, p * narrow:(p + 1) * narrow] for p in range(...]
    select_n x5 -> x6, other arithmetic: 15.1 us -> 4.25 us  [step(): send = jnp.where(high, a, b)]
  transfers between devices with their start and end apart: 65 -> 66, of which waited for: 39 -> 41; matrix products, arithmetic and copies ran while one was open for 33% -> 38% of each run, Pallas kernels for 0% -> 0%
where the time goes in v2:
time: 839 us; the launch traced here: 826 us
  waiting for transfers between devices  290 us (35%)
  matrix products  193 us (23%)
  other arithmetic  134 us (16%)
  local copies, waits for them, and re-layouts  132 us (16%)
  starting transfers between devices  61.1 us (7%)
  between operations  16.9 us (2%)
    ppermute x60, waiting for transfers between devices, swap(): return lax.ppermute(values, axis, [(d, d ^ stride) for d in range(size)])  171 us
    ppermute x4, waiting for transfers between devices, shifted(): lax.ppermute(values, 'seq', [(d, (d + shift) % size) for d in range(size)])  67.5 us
    ppermute x60, starting transfers between devices, swap(): return lax.ppermute(values, axis, [(d, d ^ stride) for d in range(size)])  56.6 us
    all_gather x2, waiting for transfers between devices, gathered(): whole = lax.all_gather(flat[None], ('dp', 'seq'), axis=0, tiled=True)  51.3 us
    dot_general x9, matrix products, against(): lax.dot_general(left, right, (((1,), (1,)), ((), ())), preferred_element_...  45.6 us
    convert_element_type x30, other arithmetic, halve_rows(): return (keep.astype(jnp.float32) + got.astype(jnp.float32)).astype(wire)  36.6 us
    dot_general x8, matrix products, times(): jnp.dot(left, c, preferred_element_type=jnp.float32)  29.9 us
    convert_element_type x1, other arithmetic, attend_back(): d_scores = (probs * (d_probs - inner)).astype(jnp.bfloat16)  28.2 us
  transfers between devices with their start and end apart: 66, of which 41 were waited for; matrix products, arithmetic and copies ran while one was open for 38% of the time, Pallas kernels for 0%

profile of v2, /device:TPU:0, one launch (start us, length us, event | category | flops | bytes accessed | tf_op | source)
XLA Modules:
  0.0 826.4 jit_solution(5906283017414187307)
XLA Ops:
  31.6 4.9 collective-permute-done.4
  37.8 5.8 collective-permute-done.5
  43.8 6.6 collective-permute-done.6
  60.3 43.0 %all-gather.5.cloned.1.call-done = bf16[2304,2304]{1,0:T(8,128)(2,1)} async-done(((bf16[72,2304]{1,0:T(8,128)(2,1)}), bf16[2304,2304]{1,0:T(8,128)(2,1)}) %all-gather.5.cloned.1.call-update) | async-done | bytes 10616848 | tf_op jit(solution)/shard_map/all_gather | solution.py:234
  103.3 3.7 fusion.138
  124.8 53.5 %collective-permute-done.10 = bf16[1,512,1728]{1,2,0:T(8,128)(2,1)} collective-permute-done((bf16[1,512,1728]{1,2,0:T(8,128)(2,1)}, bf16[1,512,1728]{1,2,0:T(8,128)(2,1)}, u32[]{:S(2)}, u32[]{:S(2)}) %collective-permute-start.10) | collective-permute-done | bytes 1769504 | tf_op jit(solution)/shard_map/ppermute | solution.py:124
  178.3 7.5 pad_maximum_fusion.2
  186.3 16.0 %multiply_reduce_fusion.1 = (f32[8,1024]{1,0:T(8,128)S(1)}, f32[8,1024,1024]{1,2,0:T(8,128)}) fusion(bf16[1024,8,72]{0,2,1:T(8,128)(2,1)S(1)} %bitcast.394, bf16[1024,8,72]{0,2,1:T(8,128)(2,1)S(1)} %bitcast.392), kind=kOutput, calls=%fused_computation.6 | convolution fusion | flops 1224728576 | bytes 35946496 | tf_op jit(solution)/shard_map/bqhd,bkhd->bhqk/dot_general | solution.py:181
  202.2 13.7 %fusion = f32[8,1024]{1,0:T(8,128)S(1)} fusion(f32[8,1024,1024]{1,2,0:T(8,128)} %get-tuple-element.229, f32[8,1024]{1,0:T(8,128)S(1)} %get-tuple-element.228), kind=kLoop, calls=%fused_computation.5 | loop fusion | flops 25157632 | bytes 33619968 | tf_op jit(solution)/shard_map/reduce_sum | solution.py:184
  215.9 14.1 %fusion.63 = bf16[8,72,1024]{2,1,0:T(8,128)(2,1)S(1)} fusion(bf16[1024,8,72]{0,2,1:T(8,128)(2,1)S(1)} %bitcast.438, f32[8,1024,1024]{1,2,0:T(8,128)} %get-tuple-element.229, f32[8,1024]{1,0:T(8,128)S(1)} %fusion, f32[8,1024]{1,0:T(8,128)S(1)} %get-tuple-element.228), kind=kOutput, calls=%fused_computation.128 | convolution fusion | flops 1242103808 | bytes 35979264 | tf_op jit(solution)/shard_map/bhqk,bkhd->bqhd/dot_general | solution.py:187
  237.5 9.8 %collective-permute-done.11 = bf16[1,512,576]{1,2,0:T(8,128)(2,1)S(1)} collective-permute-done((bf16[1,512,576]{1,2,0:T(8,128)(2,1)S(1)}, bf16[1,512,576]{1,2,0:T(8,128)(2,1)S(1)}, u32[]{:S(2)}, u32[]{:S(2)}) %collective-permute-start.11) | collective-permute-done | bytes 589856 | tf_op jit(solution)/shard_map/ppermute | solution.py:124
  253.3 8.3 %all-gather.7.cloned.1.call-done = bf16[64,72,2304]{2,1,0:T(8,128)(2,1)} async-done(((bf16[2,72,2304]{2,1,0:T(8,128)(2,1)}), bf16[64,72,2304]{2,1,0:T(8,128)(2,1)}) %all-gather.7.cloned.1.call-update) | async-done | bytes 21233680 | tf_op jit(solution)/shard_map/all_gather | solution.py:234
  261.6 8.7 %fusion.136 = (bf16[16,1,1,72,2304]{4,3,2,1,0:T(8,128)(2,1)}, bf16[16,1,1,72,2304]{4,3,2,1,0:T(8,128)(2,1)}) fusion(bf16[16,2,2,72,2304]{4,3,2,1,0:T(8,128)(2,1)} %bitcast.386), kind=kLoop, calls=%fused_computation.349 | loop fusion | bytes 21233664 | tf_op jit(solution)/shard_map/slice | solution.py:260
  270.4 6.7 slice_bitcast_fusion.7
  277.1 4.7 fusion.144
  288.8 4.7 convolution_convert_fusion.3
  293.5 4.6 convolution_convert_fusion.2
  301.9 8.3 %convolution_bitcast_fusion = f32[1,512,576]{1,2,0:T(8,128)} fusion(bf16[512,4608]{1,0:T(8,128)(2,1)} %copy-done.48, bf16[4608,576]{1,0:T(8,128)(2,1)S(1)} %bitcast.416), kind=kOutput, calls=%fused_computation.146 | convolution fusion | flops 2717908992 | bytes 11206656 | tf_op jit(solution)/shard_map/dot_general | solution.py:215
  310.2 6.0 convolution_bitcast_fusion.1
  316.2 8.8 %copy.125 = bf16[4608,576]{1,0:T(8,128)(2,1)} copy(bf16[4608,576]{0,1:T(8,128)(2,1)} %convolution_convert_fusion.2) | data formatting | bytes 10616832 | tf_op jit(solution)/shard_map/convert_element_type | solution.py:227
  325.0 8.4 %copy.124 = bf16[4608,576]{1,0:T(8,128)(2,1)} copy(bf16[4608,576]{0,1:T(8,128)(2,1)} %convolution_convert_fusion.3) | data formatting | bytes 10616832 | tf_op jit(solution)/shard_map/convert_element_type | solution.py:227
  333.4 3.9 dynamic-slice_bitcast_fusion.1
  341.6 7.5 fusion.83
  349.1 17.2 %convert_reduce_fusion = (f32[4608]{0:T(1024)}, bf16[512,4608]{1,0:T(8,128)(2,1)}) fusion(f32[4608]{0:T(1024)S(1)} %copy-done.88, f32[512,2304]{1,0:T(8,128)} %copy-done.46, f32[512,2304]{1,0:T(8,128)} %copy-done.47, f32[512,4608]{1,0:T(8,128)} %fusion.83, bf16[4608,576]{1,0:T(8,128)(2,1)} %bitcast.417, bf16[512,1152]{0,1:T(8,128)(2,1)S(1)} %copy-done.79), kind=kOutput, calls=%fused_computation.27 | convolution fusion | flops 2776886784 | bytes 29530112 | tf_op jit(solution)/shard_map/dot_general | solution.py:28
  369.9 4.5 fusion.19
  385.5 4.7 fusion.45
  390.3 6.0 fusion.42
  419.8 3.7 convolution_convert_fusion.6
  426.3 4.2 collective-permute-done.14
  435.0 14.8 %collective-permute-done.19 = bf16[2,2,288,576]{3,2,1,0:T(8,128)(2,1)} collective-permute-done((bf16[2,2,288,576]{3,2,1,0:T(8,128)(2,1)}, bf16[2,2,288,576]{3,2,1,0:T(8,128)(2,1)}, u32[]{:S(2)}, u32[]{:S(2)}) %collective-permute-start.19) | collective-permute-done | bytes 1327136 | tf_op jit(solution)/shard_map/ppermute | solution.py:35
  462.2 22.8 %multiply_reduce_fusion = (f32[8,1024]{1,0:T(8,128)S(1)}, f32[8,1024,1024]{1,2,0:T(8,128)}) fusion(f32[8,1024,1024]{1,2,0:T(8,128)} %get-tuple-element.229, f32[8,1024]{1,0:T(8,128)S(1)} %copy-done.71, bf16[1024,8,72]{0,2,1:T(8,128)(2,1)S(1)} %bitcast.398, bf16[1024,8,72]{0,2,1:T(8,128)(2,1)S(1)} %bitcast.439), kind=kOutput, calls=%fused_computation.1 | convolution fusion | flops 1241505792 | bytes 69533696 | tf_op jit(solution)/shard_map/bqhd,bkhd->bhqk/dot_general | solution.py:198
  486.2 28.2 %fusion.2 = bf16[1,8,1024,1024]{2,3,1,0:T(8,128)(2,1)} fusion(f32[8,1024,1024]{1,2,0:T(8,128)} %get-tuple-element.232, f32[8,1024,1024]{1,2,0:T(8,128)} %get-tuple-element.229, f32[8,1024]{1,0:T(8,128)S(1)} %get-tuple-element.231, f32[8,1024]{1,0:T(8,128)S(1)} %copy-done.71), kind=kLoop, calls=%fused_computation.8 | loop fusion | flops 41943040 | bytes 83951616 | tf_op jit(solution)/shard_map/convert_element_type | solution.py:201
  523.9 15.2 %fusion.56 = bf16[1,1024,8,72]{1,3,2,0:T(8,128)(2,1)} fusion(bf16[1024,8,72]{0,2,1:T(8,128)(2,1)} %bitcast.399, f32[8,1024,1024]{1,2,0:T(8,128)} %get-tuple-element.229, f32[8,1024]{1,0:T(8,128)S(1)} %copy-done.71), kind=kOutput, calls=%fused_computation.127 | convolution fusion | flops 1233125376 | bytes 35946496 | tf_op jit(solution)/shard_map/bhqk,bqhd->bkhd/dot_general | solution.py:203
  539.2 5.1 collective-permute-done.23
  546.0 6.0 collective-permute-done.22
  559.5 4.4 add_convert_fusion
  563.9 12.5 %multiply_bitcast_fusion = bf16[1,1024,8,72]{1,3,2,0:T(8,128)(2,1)} fusion(bf16[1024,8,72]{0,2,1:T(8,128)(2,1)} %bitcast.395, bf16[1,8,1024,1024]{2,3,1,0:T(8,128)(2,1)} %fusion.2), kind=kOutput, calls=%fused_computation.104 | convolution fusion | flops 1209139200 | bytes 19136512 | tf_op jit(solution)/shard_map/bhqk,bqhd->bkhd/dot_general | solution.py:207
  587.9 8.8 %multiply_convert_fusion.2 = bf16[8,72,1024]{2,1,0:T(8,128)(2,1)S(1)} fusion(bf16[1024,8,72]{0,2,1:T(8,128)(2,1)S(1)} %bitcast.393, bf16[1,8,1024,1024]{2,3,1,0:T(8,128)(2,1)} %fusion.2), kind=kOutput, calls=%fused_computation.103 | convolution fusion | flops 1209139200 | bytes 19136512 | tf_op jit(solution)/shard_map/bhqk,bkhd->bqhd/dot_general | solution.py:209
  598.4 12.4 %collective-permute-done.29 = bf16[72,576]{1,0:T(8,128)(2,1)S(1)} collective-permute-done((bf16[72,576]{1,0:T(8,128)(2,1)S(1)}, bf16[72,576]{1,0:T(8,128)(2,1)S(1)}, u32[]{:S(2)}, u32[]{:S(2)}) %collective-permute-start.29) | collective-permute-done | bytes 82976 | tf_op jit(solution)/shard_map/ppermute | solution.py:35
  616.1 27.1 %collective-permute-done.31 = bf16[2,288,576]{2,1,0:T(8,128)(2,1)S(1)} collective-permute-done((bf16[2,288,576]{2,1,0:T(8,128)(2,1)S(1)}, bf16[2,288,576]{2,1,0:T(8,128)(2,1)S(1)}, u32[]{:S(2)}, u32[]{:S(2)}) %collective-permute-start.31) | collective-permute-done | bytes 663584 | tf_op jit(solution)/shard_map/ppermute | solution.py:35
  644.4 7.7 collective-permute-done.33
  652.1 5.2 collective-permute-done.32
  677.2 3.8 copy.138
  683.5 3.9 copy.137
  690.4 5.2 fusion.52
  736.9 8.1 collective-permute-done.59
  792.9 14.8 %collective-permute-done.55 = bf16[2,72,768]{2,1,0:T(8,128)(2,1)S(1)} collective-permute-done((bf16[2,72,768]{2,1,0:T(8,128)(2,1)S(1)}, bf16[2,72,768]{2,1,0:T(8,128)(2,1)S(1)}, u32[]{:S(2)}, u32[]{:S(2)}) %collective-permute-start.55) | collective-permute-done | bytes 221216 | tf_op jit(solution)/shard_map/ppermute | solution.py:35
  807.8 5.0 collective-permute-done.57
  (609 shorter events, 298.9 us)
Async XLA Ops:
  7.2 96.1 %all-gather.5.cloned.1.call-start = ((), (), s32[]{:S(2)}) async-start(), calls=%async_computation | async-start | bytes 10948608 | tf_op jit(solution)/shard_map/all_gather | solution.py:234
  10.4 251.3 %all-gather.7.cloned.1.call-start = ((), (), s32[]{:S(2)}) async-start(), calls=%async_computation.1 | async-start | bytes 21897216 | tf_op jit(solution)/shard_map/all_gather | solution.py:234
  28.5 8.0 collective-permute-start.4
  37.1 6.4 collective-permute-start.5
  43.6 6.8 collective-permute-start.6
  118.1 60.3 %collective-permute-start.10 = (bf16[1,512,1728]{1,2,0:T(8,128)(2,1)}, bf16[1,512,1728]{1,2,0:T(8,128)(2,1)}, u32[]{:S(2)}, u32[]{:S(2)}) collective-permute-start(bf16[1,512,1728]{1,2,0:T(8,128)(2,1)} %pad_maximum_fusion.5), channel_id=1, source_target_pairs={{0,1},{1,0},{2,3},{3,2},{4,5},{5,4},{6,7},{7,6},{8,9},{9,8},{10,11... | collective-permute-start | bytes 5308424 | tf_op jit(solution)/shard_map/ppermute | solution.py:124
  230.1 17.2 %collective-permute-start.11 = (bf16[1,512,576]{1,2,0:T(8,128)(2,1)S(1)}, bf16[1,512,576]{1,2,0:T(8,128)(2,1)S(1)}, u32[]{:S(2)}, u32[]{:S(2)}) collective-permute-start(bf16[1,512,576]{1,2,0:T(8,128)(2,1)S(1)} %get-tuple-element.217), channel_id=1, source_target_pairs={{0,1},{1,0},{2,3},{3,2},{4,5},{5,4},{6,7},{7,6},{8,9},{9,8},{10,11... | collective-permute-start | bytes 1769480 | tf_op jit(solution)/shard_map/ppermute | solution.py:124
  339.7 26.6 %collective-permute-start.13 = (bf16[2,2,2,288,576]{4,3,2,1,0:T(8,128)(2,1)}, bf16[2,2,2,288,576]{4,3,2,1,0:T(8,128)(2,1)}, u32[]{:S(2)}, u32[]{:S(2)}) collective-permute-start(bf16[2,2,2,288,576]{4,3,2,1,0:T(8,128)(2,1)} %dynamic-slice_bitcast_fusion), channel_id=1, source_target_pairs={{0,2},{2,0},{4,6},{6,4},{8,10},{10,8},{12,14},{14,12},{16,18},{18,... | collective-permute-start | bytes 7962632 | tf_op jit(solution)/shard_map/ppermute | solution.py:35
  339.9 30.0 %collective-permute-start.12 = (bf16[2,2,2,288,576]{4,3,2,1,0:T(8,128)(2,1)}, bf16[2,2,2,288,576]{4,3,2,1,0:T(8,128)(2,1)}, u32[]{:S(2)}, u32[]{:S(2)}) collective-permute-start(bf16[2,2,2,288,576]{4,3,2,1,0:T(8,128)(2,1)} %dynamic-slice_bitcast_fusion.1), channel_id=1, source_target_pairs={{0,2},{2,0},{4,6},{6,4},{8,10},{10,8},{12,14},{14,12},{16,18},{18,... | collective-permute-start | bytes 7962632 | tf_op jit(solution)/shard_map/ppermute | solution.py:35
  383.4 48.2 %collective-permute-start.20 = (bf16[2,2,288,576]{3,2,1,0:T(8,128)(2,1)}, bf16[2,2,288,576]{3,2,1,0:T(8,128)(2,1)}, u32[]{:S(2)}, u32[]{:S(2)}) collective-permute-start(bf16[2,2,288,576]{3,2,1,0:T(8,128)(2,1)} %dynamic-slice_bitcast_fusion.4), channel_id=1, source_target_pairs={{0,4},{2,6},{4,0},{6,2},{8,12},{10,14},{12,8},{14,10},{16,20},{18,... | collective-permute-start | bytes 3981320 | tf_op jit(solution)/shard_map/ppermute | solution.py:35
  384.9 64.9 %collective-permute-start.19 = (bf16[2,2,288,576]{3,2,1,0:T(8,128)(2,1)}, bf16[2,2,288,576]{3,2,1,0:T(8,128)(2,1)}, u32[]{:S(2)}, u32[]{:S(2)}) collective-permute-start(bf16[2,2,288,576]{3,2,1,0:T(8,128)(2,1)} %dynamic-slice_bitcast_fusion.5), channel_id=1, source_target_pairs={{0,4},{2,6},{4,0},{6,2},{8,12},{10,14},{12,8},{14,10},{16,20},{18,... | collective-permute-start | bytes 3981320 | tf_op jit(solution)/shard_map/ppermute | solution.py:35
  400.6 52.2 %collective-permute-start.16 = (bf16[2,2,2,72,2304]{4,3,2,1,0:T(8,128)(2,1)}, bf16[2,2,2,72,2304]{4,3,2,1,0:T(8,128)(2,1)}, u32[]{:S(2)}, u32[]{:S(2)}) collective-permute-start(bf16[2,2,2,72,2304]{4,3,2,1,0:T(8,128)(2,1)} %dynamic-slice_bitcast_fusion.2), channel_id=1, source_target_pairs={{0,2},{2,0},{4,6},{6,4},{8,10},{10,8},{12,14},{14,12},{16,18},{18,... | collective-permute-start | bytes 7962632 | tf_op jit(solution)/shard_map/ppermute | solution.py:35
  406.1 50.1 %collective-permute-start.15 = (bf16[2,2,2,72,2304]{4,3,2,1,0:T(8,128)(2,1)}, bf16[2,2,2,72,2304]{4,3,2,1,0:T(8,128)(2,1)}, u32[]{:S(2)}, u32[]{:S(2)}) collective-permute-start(bf16[2,2,2,72,2304]{4,3,2,1,0:T(8,128)(2,1)} %dynamic-slice_bitcast_fusion.3), channel_id=1, source_target_pairs={{0,2},{2,0},{4,6},{6,4},{8,10},{10,8},{12,14},{14,12},{16,18},{18,... | collective-permute-start | bytes 7962632 | tf_op jit(solution)/shard_map/ppermute | solution.py:35
  414.7 15.7 %collective-permute-start.14 = (bf16[1,512,576]{1,2,0:T(8,128)(2,1)}, bf16[1,512,576]{1,2,0:T(8,128)(2,1)}, u32[]{:S(2)}, u32[]{:S(2)}) collective-permute-start(bf16[1,512,576]{1,2,0:T(8,128)(2,1)} %bitcast.65), channel_id=1, source_target_pairs={{0,1},{1,0},{2,3},{3,2},{4,5},{5,4},{6,7},{7,6},{8,9},{9,8},{10,11... | collective-permute-start | bytes 1769480 | tf_op jit(solution)/shard_map/ppermute | solution.py:124
  459.0 25.9 %collective-permute-start.18 = (bf16[2,2,2,72,576]{4,3,2,1,0:T(8,128)(2,1)S(1)}, bf16[2,2,2,72,576]{4,3,2,1,0:T(8,128)(2,1)S(1)}, u32[]{:S(2)}, u32[]{:S(2)}) collective-permute-start(bf16[2,2,2,72,576]{4,3,2,1,0:T(8,128)(2,1)S(1)} %dynamic-slice_bitcast_fusion.11), channel_id=1, source_target_pairs={{0,2},{2,0},{4,6},{6,4},{8,10},{10,8},{12,14},{14,12},{16,18},{18,... | collective-permute-start | bytes 1990664 | tf_op jit(solution)/shard_map/ppermute | solution.py:35
  459.1 26.1 %collective-permute-start.17 = (bf16[2,2,2,72,576]{4,3,2,1,0:T(8,128)(2,1)S(1)}, bf16[2,2,2,72,576]{4,3,2,1,0:T(8,128)(2,1)S(1)}, u32[]{:S(2)}, u32[]{:S(2)}) collective-permute-start(bf16[2,2,2,72,576]{4,3,2,1,0:T(8,128)(2,1)S(1)} %dynamic-slice_bitcast_fusion.12), channel_id=1, source_target_pairs={{0,2},{2,0},{4,6},{6,4},{8,10},{10,8},{12,14},{14,12},{16,18},{18,... | collective-permute-start | bytes 1990664 | tf_op jit(solution)/shard_map/ppermute | solution.py:35
  461.4 98.1 %collective-permute-start.21 = (bf16[2,2,2,72,2304]{4,3,2,1,0:T(8,128)(2,1)}, bf16[2,2,2,72,2304]{4,3,2,1,0:T(8,128)(2,1)}, u32[]{:S(2)}, u32[]{:S(2)}) collective-permute-start(bf16[2,2,2,72,2304]{4,3,2,1,0:T(8,128)(2,1)} %broadcast_select_fusion), channel_id=1, source_target_pairs={{0,1},{1,0},{2,3},{3,2},{4,5},{5,4},{6,7},{7,6},{8,9},{9,8},{10,11... | collective-permute-start | bytes 7962632 | tf_op jit(solution)/shard_map/ppermute | solution.py:35
  517.1 27.1 %collective-permute-start.23 = (bf16[2,2,72,576]{3,2,1,0:T(8,128)(2,1)}, bf16[2,2,72,576]{3,2,1,0:T(8,128)(2,1)}, u32[]{:S(2)}, u32[]{:S(2)}) collective-permute-start(bf16[2,2,72,576]{3,2,1,0:T(8,128)(2,1)} %dynamic-slice_bitcast_fusion.24), channel_id=1, source_target_pairs={{0,16},{2,18},{4,20},{6,22},{8,24},{10,26},{12,28},{14,30},{16,0},... | collective-permute-start | bytes 995336 | tf_op jit(solution)/shard_map/ppermute | solution.py:35
  518.5 33.5 %collective-permute-start.22 = (bf16[2,2,72,576]{3,2,1,0:T(8,128)(2,1)}, bf16[2,2,72,576]{3,2,1,0:T(8,128)(2,1)}, u32[]{:S(2)}, u32[]{:S(2)}) collective-permute-start(bf16[2,2,72,576]{3,2,1,0:T(8,128)(2,1)} %dynamic-slice_bitcast_fusion.25), channel_id=1, source_target_pairs={{0,16},{2,18},{4,20},{6,22},{8,24},{10,26},{12,28},{14,30},{16,0},... | collective-permute-start | bytes 995336 | tf_op jit(solution)/shard_map/ppermute | solution.py:35
  521.3 34.6 %collective-permute-start.24 = (bf16[2,2,288,576]{3,2,1,0:T(8,128)(2,1)}, bf16[2,2,288,576]{3,2,1,0:T(8,128)(2,1)}, u32[]{:S(2)}, u32[]{:S(2)}) collective-permute-start(bf16[2,2,288,576]{3,2,1,0:T(8,128)(2,1)} %broadcast_select_fusion.1), channel_id=1, source_target_pairs={{0,1},{1,0},{2,3},{3,2},{4,5},{5,4},{6,7},{7,6},{8,9},{9,8},{10,11... | collective-permute-start | bytes 3981320 | tf_op jit(solution)/shard_map/ppermute | solution.py:35
  576.5 7.2 collective-permute-start.26
  576.9 8.8 %collective-permute-start.25 = (bf16[2,72,576]{2,1,0:T(8,128)(2,1)S(1)}, bf16[2,72,576]{2,1,0:T(8,128)(2,1)S(1)}, u32[]{:S(2)}, u32[]{:S(2)}) collective-permute-start(bf16[2,72,576]{2,1,0:T(8,128)(2,1)S(1)} %dynamic-slice_bitcast_fusion.30), channel_id=1, source_target_pairs={{0,8},{2,10},{4,12},{6,14},{8,0},{10,2},{12,4},{14,6},{16,24},{18,... | collective-permute-start | bytes 497672 | tf_op jit(solution)/shard_map/ppermute | solution.py:35
  578.7 33.1 %collective-permute-start.27 = (bf16[2,2,72,2304]{3,2,1,0:T(8,128)(2,1)S(1)}, bf16[2,2,72,2304]{3,2,1,0:T(8,128)(2,1)S(1)}, u32[]{:S(2)}, u32[]{:S(2)}) collective-permute-start(bf16[2,2,72,2304]{3,2,1,0:T(8,128)(2,1)S(1)} %dynamic-slice_bitcast_fusion.6), channel_id=1, source_target_pairs={{0,4},{2,6},{4,0},{6,2},{8,12},{10,14},{12,8},{14,10},{16,20},{18,... | collective-permute-start | bytes 3981320 | tf_op jit(solution)/shard_map/ppermute | solution.py:35
  585.8 25.0 %collective-permute-start.29 = (bf16[72,576]{1,0:T(8,128)(2,1)S(1)}, bf16[72,576]{1,0:T(8,128)(2,1)S(1)}, u32[]{:S(2)}, u32[]{:S(2)}) collective-permute-start(bf16[72,576]{1,0:T(8,128)(2,1)S(1)} %dynamic-slice_bitcast_fusion.34), channel_id=1, source_target_pairs={{0,4},{2,6},{4,0},{6,2},{8,12},{10,14},{12,8},{14,10},{16,20},{18,... | collective-permute-start | bytes 248840 | tf_op jit(solution)/shard_map/ppermute | solution.py:35
  587.3 24.5 %collective-permute-start.28 = (bf16[72,576]{1,0:T(8,128)(2,1)S(1)}, bf16[72,576]{1,0:T(8,128)(2,1)S(1)}, u32[]{:S(2)}, u32[]{:S(2)}) collective-permute-start(bf16[72,576]{1,0:T(8,128)(2,1)S(1)} %dynamic-slice_bitcast_fusion.35), channel_id=1, source_target_pairs={{0,4},{2,6},{4,0},{6,2},{8,12},{10,14},{12,8},{14,10},{16,20},{18,... | collective-permute-start | bytes 248840 | tf_op jit(solution)/shard_map/ppermute | solution.py:35
  596.8 46.4 %collective-permute-start.31 = (bf16[2,288,576]{2,1,0:T(8,128)(2,1)S(1)}, bf16[2,288,576]{2,1,0:T(8,128)(2,1)S(1)}, u32[]{:S(2)}, u32[]{:S(2)}) collective-permute-start(bf16[2,288,576]{2,1,0:T(8,128)(2,1)S(1)} %dynamic-slice_bitcast_fusion.10), channel_id=1, source_target_pairs={{0,16},{2,18},{4,20},{6,22},{8,24},{10,26},{12,28},{14,30},{16,0},... | collective-permute-start | bytes 1990664 | tf_op jit(solution)/shard_map/ppermute | solution.py:35
  612.4 45.9 %collective-permute-start.30 = (bf16[1,512,1728]{1,2,0:T(8,128)(2,1)S(1)}, bf16[1,512,1728]{1,2,0:T(8,128)(2,1)S(1)}, u32[]{:S(2)}, u32[]{:S(2)}) collective-permute-start(bf16[1,512,1728]{1,2,0:T(8,128)(2,1)S(1)} %pad_maximum_fusion.3), channel_id=1, source_target_pairs={{0,1},{1,0},{2,3},{3,2},{4,5},{5,4},{6,7},{7,6},{8,9},{9,8},{10,11... | collective-permute-start | bytes 5308424 | tf_op jit(solution)/shard_map/ppermute | solution.py:124
  613.5 43.8 %collective-permute-start.32 = (bf16[2,72,2304]{2,1,0:T(8,128)(2,1)S(1)}, bf16[2,72,2304]{2,1,0:T(8,128)(2,1)S(1)}, u32[]{:S(2)}, u32[]{:S(2)}) collective-permute-start(bf16[2,72,2304]{2,1,0:T(8,128)(2,1)S(1)} %dynamic-slice_bitcast_fusion.13), channel_id=1, source_target_pairs={{0,16},{2,18},{4,20},{6,22},{8,24},{10,26},{12,28},{14,30},{16,0},... | collective-permute-start | bytes 1990664 | tf_op jit(solution)/shard_map/ppermute | solution.py:35
  615.1 37.0 %collective-permute-start.33 = (bf16[72,576]{1,0:T(8,128)(2,1)S(1)}, bf16[72,576]{1,0:T(8,128)(2,1)S(1)}, u32[]{:S(2)}, u32[]{:S(2)}) collective-permute-start(bf16[72,576]{1,0:T(8,128)(2,1)S(1)} %broadcast_select_fusion.4), channel_id=1, source_target_pairs={{0,1},{1,0},{2,3},{3,2},{4,5},{5,4},{6,7},{7,6},{8,9},{9,8},{10,11... | collective-permute-start | bytes 248840 | tf_op jit(solution)/shard_map/ppermute | solution.py:35
  673.4 29.0 %collective-permute-start.39 = (bf16[72,2304]{1,0:T(8,128)(2,1)}, bf16[72,2304]{1,0:T(8,128)(2,1)}, u32[]{:S(2)}, u32[]{:S(2)}) collective-permute-start(bf16[72,2304]{1,0:T(8,128)(2,1)} %dynamic-slice_bitcast_fusion.26), channel_id=1, source_target_pairs={{0,8},{2,10},{4,12},{6,14},{8,0},{10,2},{12,4},{14,6},{16,24},{18,... | collective-permute-start | bytes 995336 | tf_op jit(solution)/shard_map/ppermute | solution.py:35
  675.2 29.6 %collective-permute-start.38 = (bf16[288,576]{1,0:T(8,128)(2,1)}, bf16[288,576]{1,0:T(8,128)(2,1)}, u32[]{:S(2)}, u32[]{:S(2)}) collective-permute-start(bf16[288,576]{1,0:T(8,128)(2,1)} %dynamic-slice_bitcast_fusion.23), channel_id=1, source_target_pairs={{0,8},{2,10},{4,12},{6,14},{8,0},{10,2},{12,4},{14,6},{16,24},{18,... | collective-permute-start | bytes 995336 | tf_op jit(solution)/shard_map/ppermute | solution.py:35
  699.5 7.3 collective-permute-start.35
  699.6 7.0 collective-permute-start.34
  701.2 5.8 collective-permute-start.37
  715.3 11.4 %collective-permute-start.40 = (f32[1,6912]{1,0:T(1,128)S(1)}, f32[1,6912]{1,0:T(1,128)S(1)}, u32[]{:S(2)}, u32[]{:S(2)}) collective-permute-start(f32[1,6912]{1,0:T(1,128)S(1)} %constant_dynamic-update-slice_fusion), channel_id=1, source_target_pairs={{0,1},{1,0},{2,3},{3,2},{4,5},{5,4},{6,7},{7,6},{8,9},{9,8},{10,11... | collective-permute-start | bytes 82952 | tf_op jit(solution)/shard_map/ppermute | solution.py:35
  720.1 40.8 %collective-permute-start.47 = (bf16[2,2,72,960]{3,2,1,0:T(8,128)(2,1)}, bf16[2,2,72,960]{3,2,1,0:T(8,128)(2,1)}, u32[]{:S(2)}, u32[]{:S(2)}) collective-permute-start(bf16[2,2,72,960]{3,2,1,0:T(8,128)(2,1)} %dynamic-slice_bitcast_fusion.14), channel_id=1, source_target_pairs={{0,4},{2,6},{4,0},{6,2},{8,12},{10,14},{12,8},{14,10},{16,20},{18,... | collective-permute-start | bytes 1658888 | tf_op jit(solution)/shard_map/ppermute | solution.py:35
  721.5 40.8 %collective-permute-start.46 = (bf16[2,2,72,960]{3,2,1,0:T(8,128)(2,1)}, bf16[2,2,72,960]{3,2,1,0:T(8,128)(2,1)}, u32[]{:S(2)}, u32[]{:S(2)}) collective-permute-start(bf16[2,2,72,960]{3,2,1,0:T(8,128)(2,1)} %dynamic-slice_bitcast_fusion.15), channel_id=1, source_target_pairs={{0,4},{2,6},{4,0},{6,2},{8,12},{10,14},{12,8},{14,10},{16,20},{18,... | collective-permute-start | bytes 1658888 | tf_op jit(solution)/shard_map/ppermute | solution.py:35
  723.3 40.6 %collective-permute-start.45 = (bf16[2,2,2,72,768]{4,3,2,1,0:T(8,128)(2,1)}, bf16[2,2,2,72,768]{4,3,2,1,0:T(8,128)(2,1)}, u32[]{:S(2)}, u32[]{:S(2)}) collective-permute-start(bf16[2,2,2,72,768]{4,3,2,1,0:T(8,128)(2,1)} %broadcast_select_fusion.2), channel_id=1, source_target_pairs={{0,1},{1,0},{2,3},{3,2},{4,5},{5,4},{6,7},{7,6},{8,9},{9,8},{10,11... | collective-permute-start | bytes 2654216 | tf_op jit(solution)/shard_map/ppermute | solution.py:35
  736.0 9.0 %collective-permute-start.59 = (f32[2,2,2,2,1,504]{5,4,3,2,1,0:T(1,128)S(1)}, f32[2,2,2,2,1,504]{5,4,3,2,1,0:T(1,128)S(1)}, u32[]{:S(2)}, u32[]{:S(2)}) collective-permute-start(f32[2,2,2,2,1,504]{5,4,3,2,1,0:T(1,128)S(1)} %bitcast.452), channel_id=1, source_target_pairs={{0,1},{1,0},{2,3},{3,2},{4,5},{5,4},{6,7},{7,6},{8,9},{9,8},{10,11... | collective-permute-start | bytes 96776 | tf_op jit(solution)/shard_map/ppermute | solution.py:35
  736.8 8.5 %collective-permute-start.41 = (bf16[1,3456]{1,0:T(2,128)(2,1)S(1)}, bf16[1,3456]{1,0:T(2,128)(2,1)S(1)}, u32[]{:S(2)}, u32[]{:S(2)}) collective-permute-start(bf16[1,3456]{1,0:T(2,128)(2,1)S(1)} %constant_dynamic-slice_fusion.9), channel_id=1, source_target_pairs={{0,2},{2,0},{4,6},{6,4},{8,10},{10,8},{12,14},{14,12},{16,18},{18,... | collective-permute-start | bytes 20744 | tf_op jit(solution)/shard_map/ppermute | solution.py:35
  755.1 5.7 collective-permute-start.44
  771.3 12.6 %collective-permute-start.53 = (bf16[2,2,72,768]{3,2,1,0:T(8,128)(2,1)}, bf16[2,2,72,768]{3,2,1,0:T(8,128)(2,1)}, u32[]{:S(2)}, u32[]{:S(2)}) collective-permute-start(bf16[2,2,72,768]{3,2,1,0:T(8,128)(2,1)} %dynamic-slice_bitcast_fusion.22), channel_id=1, source_target_pairs={{0,4},{2,6},{4,0},{6,2},{8,12},{10,14},{12,8},{14,10},{16,20},{18,... | collective-permute-start | bytes 1327112 | tf_op jit(solution)/shard_map/ppermute | solution.py:35
  774.7 14.0 %collective-permute-start.54 = (bf16[2,2,72,960]{3,2,1,0:T(8,128)(2,1)S(1)}, bf16[2,2,72,960]{3,2,1,0:T(8,128)(2,1)S(1)}, u32[]{:S(2)}, u32[]{:S(2)}) collective-permute-start(bf16[2,2,72,960]{3,2,1,0:T(8,128)(2,1)S(1)} %broadcast_select_fusion.3), channel_id=1, source_target_pairs={{0,1},{1,0},{2,3},{3,2},{4,5},{5,4},{6,7},{7,6},{8,9},{9,8},{10,11... | collective-permute-start | bytes 1658888 | tf_op jit(solution)/shard_map/ppermute | solution.py:35
  778.2 5.7 collective-permute-start.52
  789.2 18.5 %collective-permute-start.55 = (bf16[2,72,768]{2,1,0:T(8,128)(2,1)S(1)}, bf16[2,72,768]{2,1,0:T(8,128)(2,1)S(1)}, u32[]{:S(2)}, u32[]{:S(2)}) collective-permute-start(bf16[2,72,768]{2,1,0:T(8,128)(2,1)S(1)} %dynamic-slice_bitcast_fusion.28), channel_id=1, source_target_pairs={{0,16},{2,18},{4,20},{6,22},{8,24},{10,26},{12,28},{14,30},{16,0},... | collective-permute-start | bytes 663560 | tf_op jit(solution)/shard_map/ppermute | solution.py:35
  791.8 21.0 %collective-permute-start.57 = (bf16[2,72,960]{2,1,0:T(8,128)(2,1)S(1)}, bf16[2,72,960]{2,1,0:T(8,128)(2,1)S(1)}, u32[]{:S(2)}, u32[]{:S(2)}) collective-permute-start(bf16[2,72,960]{2,1,0:T(8,128)(2,1)S(1)} %dynamic-slice_bitcast_fusion.27), channel_id=1, source_target_pairs={{0,16},{2,18},{4,20},{6,22},{8,24},{10,26},{12,28},{14,30},{16,0},... | collective-permute-start | bytes 829448 | tf_op jit(solution)/shard_map/ppermute | solution.py:35
  807.7 7.4 collective-permute-start.56
  812.9 5.3 collective-permute-start.58
  (148 other events, 1939.7 us)
Sparse Core Ops, SparseCore 0:
  11.5 91.7 all-gather.4
  106.8 154.8 all-gather.6
